TPU v7x, 32 devices: a whole 2x2x4 slice. The times are simulated.
32 devices in a mesh: op: 16 (over z, y, x), sec: 2 (over core).
Axes of the slice: x: 2, y: 2, z: 4, core: 2. Of those that a mesh axis runs over, the one named last changes fastest.
Arguments:
- wavefunction: bfloat16 [2, 512, 512], P('sec', 'op'), may hold values from -6 to 6
- left_ops: bfloat16 [128, 512, 512], P(('op', 'sec')), may hold values from -0.25 to 0.25
- right_ops: bfloat16 [128, 512, 512], P(('op', 'sec')), may hold values from -0.25 to 0.25
- in_sector: int32 [128], P(('op', 'sec')), may hold values from 0 to 1
- counts: int32 [16, 2], replicated, may hold values from 1 to 4
Outputs:
- applied: bfloat16 [2, 512, 512], P('sec', 'op')
Inputs may be any that keep to these rules, and one draw needn't show every extreme that they name: `counts`: a device's live terms are its first slots, as many as its count.
All inputs are finite; a program needn't handle non-finite values.
Results may differ from a plain program's by a relative error of at most 0.0049.
Values may be sent and summed in bfloat16 or wider, within the bound.
No kernel may reach another device: no remote copies, remote signals or barrier semaphores. Data moves between devices by JAX's collectives and lax.ppermute only.
A program may use at most 64 MiB of HBM per device.

v0:
```python
import jax
import jax.numpy as jnp
from jax import lax
from jax.sharding import PartitionSpec as P


def shards(wavefunction, left_ops, right_ops, in_sector, counts):
    op_devices = lax.axis_size("op")
    op_place = lax.axis_index("op")
    sec_place = lax.axis_index("sec")
    by_rows = lax.all_gather(wavefunction, "op", axis=1, tiled=True)
    gathered = lax.all_gather(by_rows, "sec", axis=0, tiled=True)

    def block_of(slot_index):
        sector = lax.dynamic_index_in_dim(in_sector, slot_index, 0, keepdims=False)
        return lax.dynamic_index_in_dim(gathered, sector, 0, keepdims=False)

    own_count = counts[op_place, sec_place]

    def local_step(slot_index, summed):
        left_block = lax.dynamic_index_in_dim(left_ops, slot_index, 0, keepdims=False)
        right_block = lax.dynamic_index_in_dim(right_ops, slot_index, 0, keepdims=False)
        halfway = jnp.dot(
            left_block, block_of(slot_index), preferred_element_type=jnp.float32
        ).astype(jnp.bfloat16)
        product = lax.dot_general(
            halfway, right_block, (((1,), (1,)), ((), ())), preferred_element_type=jnp.float32
        )
        return summed + product

    initial = jnp.zeros((left_ops.shape[1], right_ops.shape[1]), jnp.float32)
    summed = lax.fori_loop(0, own_count, local_step, initial)
    shares = lax.psum_scatter(summed, "op", scatter_dimension=0, tiled=True)
    factor = (op_devices * left_ops.shape[0]) ** (-0.5)
    return (shares * factor).astype(jnp.bfloat16)[None]


def solution(mesh):
    placed = (
        P("sec", "op", None),
        P(("op", "sec"), None, None),
        P(("op", "sec"), None, None),
        P(("op", "sec")),
        P(),
    )
    return jax.shard_map(
        shards, mesh=mesh, in_specs=placed, out_specs=P("sec", "op", None), check_vma=False
    )
```

profile of v0, /device:TPU:0, one launch (start us, length us, event | category | flops | bytes accessed | tf_op | source)
XLA Modules:
  0.0 169.9 jit_solution(8849296340973981867)
XLA Ops:
  6.5 0.0 copy-start.1
  6.5 0.0 all-gather.2.cloned.1.call-start
  6.5 48.2 %all_gather.6 = bf16[1,512,512]{2,1,0:T(8,128)(2,1)} all-gather(bf16[1,32,512]{2,1,0:T(8,128)(2,1)} %param.7), channel_id=1, replica_groups=mesh['op'=16,'sec'=2] {'op'}, dimensions={1}, use_global_device_ids=true | all-gather | bytes 557056 | tf_op jit(solution)/shard_map/all_gather | solution.py:11
  54.7 0.0 all-gather.2.cloned.1.call-update
  54.7 0.0 reduce-scatter.2.cloned.1.call-start
  54.8 1.3 dynamic_slice.18
  56.1 3.7 %all-gather.2.cloned.1.call-done = bf16[2,512,512]{2,1,0:T(8,128)(2,1)} async-done(((bf16[1,512,512]{2,1,0:T(8,128)(2,1)}), bf16[2,512,512]{2,1,0:T(8,128)(2,1)}) %all-gather.2.cloned.1.call-update) | async-done | bytes 1048592 | tf_op jit(solution)/shard_map/all_gather | solution.py:12
  59.8 0.1 broadcast_in_dim.6
  59.9 0.0 copy-done.1
  59.9 5.9 %while.10 = (s32[]{:T(128)}, f32[512,512]{1,0:T(8,128)S(1)}, s32[]{:T(128)}, bf16[4,512,512]{2,1,0:T(8,128)(2,1)}, s32[4]{0:T(128)S(1)}, /*index=5*/bf16[2,512,5...) while((s32[]{:T(128)}, f32[512,512]{1,0:T(8,128)S(1)}, ...), condition=%wide.region_1.2_spmd, body=%wide.region_0.1_spmd.sunk | while | flops 537395200 | bytes 3671749 | solution.py:32
  60.6 0.6 dynamic_slice.40
  63.1 2.1 %convolution_add_fusion.2 = f32[512,512]{1,0:T(8,128)S(1)} fusion(f32[512,512]{1,0:T(8,128)S(1)} %get-tuple-element.114, bf16[4,512,512]{2,1,0:T(8,128)(2,1)} %get-tuple-element.130, s32[]{:T(128)S(6)} %select_n.21, bf16[2,512,512]{2,1,0:T(8,128)(2,1)} %get-tuple-element.129, s32[]{:T(128)S(6)} %select_n.22, bf16[4,512,512]{2,1,0:T(8,128)(2,1)} %get-tuple-element.127), kind=kOutput, calls=%fused_computation.clone.1 | convolution fusion | flops 537395200 | bytes 3671552 | tf_op jit(solution)/shard_map/while/body/dot_general | solution.py:26
  65.8 0.0 copy-start
  65.9 1.0 copy-done
  66.8 0.0 reduce-scatter.2.cloned.1.call-update
  66.8 94.8 %reduce-scatter.2.cloned.1.call-done = f32[32,512]{1,0:T(8,128)} async-done(((f32[512,512]{1,0:T(8,128)}), f32[32,512]{1,0:T(8,128)}) %reduce-scatter.2.cloned.1.call-update) | async-done | bytes 65552 | tf_op jit(solution)/shard_map/reduce_scatter | solution.py:33
  161.6 1.5 fusion.12
Async XLA Ops:
  6.5 53.4 %copy-start.1 = (s32[4]{0:T(128)S(1)}, s32[4]{0:T(128)}, u32[]{:S(2)}) copy-start(s32[4]{0:T(128)} %param.10) | copy-start | bytes 52
  6.5 53.3 %all-gather.2.cloned.1.call-start = ((), (), s32[]{:S(2)}) async-start(), calls=%async_computation.1 | async-start | bytes 1572864 | tf_op jit(solution)/shard_map/all_gather | solution.py:12
  54.7 106.9 %reduce-scatter.2.cloned.1.call-start = ((), (), s32[]{:S(2)}) async-start(), calls=%async_computation.2 | async-start | bytes 1114112 | tf_op jit(solution)/shard_map/reduce_scatter | solution.py:33
  65.8 1.0 copy-start
Sparse Core Ops, SparseCore 0:
  54.9 4.8 all-gather.1
  67.0 94.6 reduce-scatter.1
where the time goes:
time: 170 us
  waiting for transfers between devices  98.5 us (58%)
  blocking collectives  48.2 us (28%)
  between operations  13.4 us (8%)
  loops' own time  3.2 us (2%)
  local copies, waits for them, and re-layouts  3.02 us (2%)
  matrix products  2.1 us (1%)
    reduce_scatter x1, waiting for transfers between devices, shards(): shares = lax.psum_scatter(summed, 'op', scatter_dimension=0, tiled=True)  94.8 us
    all_gather x1, blocking collectives, shards(): by_rows = lax.all_gather(wavefunction, 'op', axis=1, tiled=True)  48.2 us
    all_gather x1, waiting for transfers between devices, shards(): gathered = lax.all_gather(by_rows, 'sec', axis=0, tiled=True)  3.67 us
  transfers between devices with their start and end apart: 2, of which 2 were waited for; matrix products, arithmetic and copies ran while one was open for 1% of the time, Pallas kernels for 0%

commit v1 on v0

v1 whole, which is shorter than its diff:
```python
import functools

import jax
import jax.numpy as jnp
from jax import lax
from jax.experimental import pallas as pl
from jax.experimental.pallas import tpu as pltpu
from jax.sharding import PartitionSpec as P


def exchange(value, axis, mask):
    size = lax.axis_size(axis)
    return lax.ppermute(value, axis, [(i, i ^ mask) for i in range(size)])


def spread(position, masks):
    return sum(mask for bit, mask in enumerate(masks) if position >> bit & 1)


def unfold(gathered, place, masks):
    bits = len(masks)
    folded = gathered.reshape((2,) * bits + (-1, gathered.shape[1]))
    for bit, mask in enumerate(masks):
        there = (place & mask) != 0
        folded = jnp.where(there, jnp.flip(folded, bits - 1 - bit), folded)
    return folded.transpose(tuple(range(bits))[::-1] + (bits, bits + 1)).reshape(gathered.shape)


def terms_kernel(blocks, sizes, home_ref, away_ref, sector_ref, count_ref, *refs):
    sectors, pieces = sizes
    piece_refs, refs = refs[: sectors * pieces], refs[sectors * pieces :]
    left_ref, right_ref, keep_ref, send_ref, wave, ordered = refs
    for sector in range(sectors):
        first = 0
        for piece in range(pieces):
            ref = piece_refs[sector * pieces + piece]
            for part in range(ref.shape[0] // blocks):
                start = pl.multiple_of(away_ref[first] * blocks, blocks)
                wave[home_ref[home_ref.shape[0] - sectors + sector], pl.ds(start, blocks), :] = ref[
                    part * blocks : (part + 1) * blocks, :
                ]
                first += 1
    slots = left_ref.shape[0]
    total = None
    for slot in range(slots):
        halfway = jnp.dot(
            left_ref[slot], wave[sector_ref[slot]], preferred_element_type=jnp.float32
        ).astype(jnp.bfloat16)
        halfway = jnp.where(slot < count_ref[0], halfway, jnp.zeros_like(halfway))
        product = lax.dot_general(
            halfway, right_ref[slot], (((1,), (1,)), ((), ())), preferred_element_type=jnp.float32
        )
        total = product if total is None else total + product
    share = keep_ref.shape[0] * 2 // (home_ref.shape[0] - sectors)
    for block in range(home_ref.shape[0] - sectors):
        start = pl.multiple_of(home_ref[block] * share, share)
        ordered[pl.ds(start, share), :] = total[block * share : (block + 1) * share, :]
    half = keep_ref.shape[0]
    keep_ref[...] = ordered[:half, :]
    send_ref[...] = ordered[half:, :].astype(jnp.bfloat16)


def shards(wavefunction, left_ops, right_ops, in_sector, counts):
    op_devices, sec_devices = lax.axis_size("op"), lax.axis_size("sec")
    op_place, sec_place = lax.axis_index("op"), lax.axis_index("sec")
    slots, left_rows, order = left_ops.shape
    near = [1 << bit for bit in range(op_devices.bit_length() - 1)]
    far = near[::-1]

    held = wavefunction[0]
    pieces = [held]
    for step, mask in enumerate(far):
        arrived = exchange(held, "op", mask)
        pieces.append(arrived)
        if step < len(far) - 1:
            held = jnp.concatenate([held, arrived], axis=0)
    by_sector = [pieces]
    for mask in range(1, sec_devices):
        by_sector.append([exchange(piece, "sec", mask) for piece in pieces])

    away = op_place ^ jnp.array([spread(p, far) for p in range(op_devices)], jnp.int32)
    inverse = [0] * op_devices
    for position in range(op_devices):
        inverse[spread(position, near[::-1])] = position
    home = jnp.array(inverse, jnp.int32)[op_place ^ jnp.arange(op_devices)]
    places = sec_place ^ jnp.arange(sec_devices, dtype=jnp.int32)
    home = jnp.concatenate([home, places])
    count = lax.dynamic_slice(counts, (op_place, sec_place), (1, 1))[0]

    blocks = held.shape[0] * 2 // op_devices
    if blocks % 16:
        by_sector = [[unfold(jnp.concatenate(group, axis=0), op_place, far)] for group in by_sector]
        blocks, away = order, jnp.zeros((1,), jnp.int32)
    flat = [piece for group in by_sector for piece in group]
    smem, vmem = pl.BlockSpec(memory_space=pltpu.SMEM), pl.BlockSpec(memory_space=pltpu.VMEM)
    half = left_rows // 2
    keep, send = pl.pallas_call(
        functools.partial(terms_kernel, blocks, (sec_devices, len(by_sector[0]))),
        out_shape=(
            jax.ShapeDtypeStruct((half, order), jnp.float32),
            jax.ShapeDtypeStruct((half, order), jnp.bfloat16),
        ),
        in_specs=[smem] * 4 + [vmem] * (len(flat) + 2),
        out_specs=(vmem, vmem),
        scratch_shapes=[
            pltpu.VMEM((sec_devices, order, order), jnp.bfloat16),
            pltpu.VMEM((left_rows, order), jnp.float32),
        ],
        compiler_params=pltpu.CompilerParams(vmem_limit_bytes=32 * 2**20),
        cost_estimate=pl.CostEstimate(
            flops=4 * slots * left_rows * order * order,
            bytes_accessed=4 * slots * left_rows * order,
            transcendentals=0,
        ),
    )(home, away, in_sector, count, *flat, left_ops, right_ops)

    for mask in near[:-1]:
        arrived = exchange(send, "op", mask).astype(jnp.float32)
        half //= 2
        send = (keep[half:] + arrived[half:]).astype(jnp.bfloat16)
        keep = keep[:half] + arrived[:half]
    shares = keep + exchange(send, "op", near[-1]).astype(jnp.float32)
    factor = (op_devices * slots) ** (-0.5)
    return (shares * factor).astype(jnp.bfloat16)[None]


def solution(mesh):
    placed = (
        P("sec", "op", None),
        P(("op", "sec"), None, None),
        P(("op", "sec"), None, None),
        P(("op", "sec")),
        P(),
    )
    return jax.shard_map(
        shards, mesh=mesh, in_specs=placed, out_specs=P("sec", "op", None), check_vma=False
    )
```

time: 170 us -> 60.6 us (0.36)
  waiting for transfers between devices: 98.5 us -> 26.8 us
  blocking collectives: 48.2 us -> 0 us
  starting transfers between devices: 0.04 us -> 18.4 us
  between operations: 13.4 us -> 0.1 us
  local copies, waits for them, and re-layouts: 3.02 us -> 7.16 us
  Pallas kernels: 0 us -> 3.67 us
  loops' own time: 3.2 us -> 0 us
  other arithmetic: 1.46 us -> 3.91 us
  matrix products: 2.1 us -> 0 us
    reduce_scatter x1 -> x0, waiting for transfers between devices: 94.8 us -> none  [shards(): shares = lax.psum_scatter(summed, 'op', scatter_dimension=0, tiled=True)]
    all_gather x1 -> x0, blocking collectives: 48.2 us -> none  [shards(): by_rows = lax.all_gather(wavefunction, 'op', axis=1, tiled=True)]
    ppermute x0 -> x13, waiting for transfers between devices: none -> 26.8 us  [exchange(): return lax.ppermute(value, axis, [(i, i ^ mask) for i in range(size)])]
    ppermute x0 -> x13, starting transfers between devices: none -> 18.4 us  [exchange(): return lax.ppermute(value, axis, [(i, i ^ mask) for i in range(size)])]
    all_gather x1 -> x0, waiting for transfers between devices: 3.67 us -> none  [shards(): gathered = lax.all_gather(by_rows, 'sec', axis=0, tiled=True)]
    pallas_call x0 -> x1, Pallas kernels: none -> 3.67 us  [shards(): pl.pallas_call(functools.partial(terms_kernel, blocks, (sec_devices, len(...]
    unnamed x4 -> x8, local copies, waits for them, and re-layouts: 0.97 us -> 4.59 us
    another operation x1 -> x0, loops' own time: 3.2 us -> none  [shards(): summed = lax.fori_loop(0, own_count, local_step, initial)]
  transfers between devices with their start and end apart: 2 -> 13, of which waited for: 2 -> 8; matrix products, arithmetic and copies ran while one was open for 1% -> 7% of each run, Pallas kernels for 0% -> 0%
where the time goes in v1:
time: 60.6 us; the launch traced here: 60.1 us
  waiting for transfers between devices  26.8 us (44%)
  starting transfers between devices  18.4 us (30%)
  local copies, waits for them, and re-layouts  7.16 us (12%)
  other arithmetic  3.91 us (6%)
  Pallas kernels  3.67 us (6%)
    ppermute x13, waiting for transfers between devices, exchange(): return lax.ppermute(value, axis, [(i, i ^ mask) for i in range(size)])  26.8 us
    ppermute x13, starting transfers between devices, exchange(): return lax.ppermute(value, axis, [(i, i ^ mask) for i in range(size)])  18.4 us
    unnamed x8, local copies, waits for them, and re-layouts  4.59 us
    pallas_call x1, Pallas kernels, shards(): pl.pallas_call(functools.partial(terms_kernel, blocks, (sec_devices, len(...  3.67 us
    concatenate x3, other arithmetic, shards(): held = jnp.concatenate([held, arrived], axis=0)  2.3 us
    gather x1, local copies, waits for them, and re-layouts, shards(): home = jnp.array(inverse, jnp.int32)[op_place ^ jnp.arange(op_devices)]  1.31 us
    dynamic_slice x1, local copies, waits for them, and re-layouts, shards(): count = lax.dynamic_slice(counts, (op_place, sec_place), (1, 1))[0]  1.26 us
  transfers between devices with their start and end apart: 13, of which 8 were waited for; matrix products, arithmetic and copies ran while one was open for 7% of the time, Pallas kernels for 0%

profile of v1, /device:TPU:0, one launch (start us, length us, event | category | flops | bytes accessed | tf_op | source)
XLA Modules:
  0.0 60.1 jit_solution(3303883151059327324)
XLA Ops:
  0.0 4.0 %collective-permute-start = (bf16[32,512]{1,0:T(8,128)(2,1)}, bf16[32,512]{1,0:T(8,128)(2,1)S(1)}, u32[]{:S(2)}, u32[]{:S(2)}) collective-permute-start(bf16[32,512]{1,0:T(8,128)(2,1)} %bitcast.6), channel_id=1, source_target_pairs={{0,16},{2,18},{4,20},{6,22},{8,24},{10,26},{12,28},{14,30},{16,0},... | collective-permute-start | bytes 98312 | tf_op jit(solution)/shard_map/ppermute | solution.py:13
  4.0 2.5 %collective-permute-done.refs_1_ = bf16[32,512]{1,0:T(8,128)(2,1)S(1)} collective-permute-done((bf16[32,512]{1,0:T(8,128)(2,1)}, bf16[32,512]{1,0:T(8,128)(2,1)S(1)}, u32[]{:S(2)}, u32[]{:S(2)}) %collective-permute-start) | collective-permute-done | bytes 32800 | tf_op jit(solution)/shard_map/ppermute | solution.py:13
  6.5 0.8 %pad_maximum_fusion.2 = bf16[64,512]{1,0:T(8,128)(2,1)S(1)} fusion(bf16[32,512]{1,0:T(8,128)(2,1)S(1)} %collective-permute-done.refs_1_, bf16[32,512]{1,0:T(8,128)(2,1)} %bitcast.7), kind=kLoop, calls=%fused_computation.15 | loop fusion | flops 131072 | bytes 131072 | tf_op jit(solution)/shard_map/concatenate | solution.py:76
  7.3 1.6 %collective-permute-start.1 = (bf16[64,512]{1,0:T(8,128)(2,1)S(1)}, bf16[64,512]{1,0:T(8,128)(2,1)S(1)}, u32[]{:S(2)}, u32[]{:S(2)}) collective-permute-start(bf16[64,512]{1,0:T(8,128)(2,1)S(1)} %pad_maximum_fusion.2), channel_id=1, source_target_pairs={{0,8},{2,10},{4,12},{6,14},{8,0},{10,2},{12,4},{14,6},{16,24},{18,... | collective-permute-start | bytes 196616 | tf_op jit(solution)/shard_map/ppermute | solution.py:13
  8.8 2.7 %collective-permute-done.1.refs_2_ = bf16[64,512]{1,0:T(8,128)(2,1)S(1)} collective-permute-done((bf16[64,512]{1,0:T(8,128)(2,1)S(1)}, bf16[64,512]{1,0:T(8,128)(2,1)S(1)}, u32[]{:S(2)}, u32[]{:S(2)}) %collective-permute-start.1) | collective-permute-done | bytes 65568 | tf_op jit(solution)/shard_map/ppermute | solution.py:13
  11.5 0.8 %pad_maximum_fusion.1 = bf16[128,512]{1,0:T(8,128)(2,1)S(1)} fusion(bf16[64,512]{1,0:T(8,128)(2,1)S(1)} %collective-permute-done.1.refs_2_, bf16[32,512]{1,0:T(8,128)(2,1)S(1)} %collective-permute-done.refs_1_, bf16[32,512]{1,0:T(8,128)(2,1)} %bitcast.8), kind=kLoop, calls=%fused_computation.8 | loop fusion | flops 393216 | bytes 262144 | tf_op jit(solution)/shard_map/concatenate | solution.py:76
  12.3 1.8 %collective-permute-start.2 = (bf16[128,512]{1,0:T(8,128)(2,1)S(1)}, bf16[128,512]{1,0:T(8,128)(2,1)S(1)}, u32[]{:S(2)}, u32[]{:S(2)}) collective-permute-start(bf16[128,512]{1,0:T(8,128)(2,1)S(1)} %pad_maximum_fusion.1), channel_id=1, source_target_pairs={{0,4},{2,6},{4,0},{6,2},{8,12},{10,14},{12,8},{14,10},{16,20},{18,... | collective-permute-start | bytes 393224 | tf_op jit(solution)/shard_map/ppermute | solution.py:13
  14.1 0.0 collective-permute-start.4
  14.1 3.2 %collective-permute-done.2.refs_3_ = bf16[128,512]{1,0:T(8,128)(2,1)S(1)} collective-permute-done((bf16[128,512]{1,0:T(8,128)(2,1)S(1)}, bf16[128,512]{1,0:T(8,128)(2,1)S(1)}, u32[]{:S(2)}, u32[]{:S(2)}) %collective-permute-start.2) | collective-permute-done | bytes 131104 | tf_op jit(solution)/shard_map/ppermute | solution.py:13
  17.3 0.8 %pad_maximum_fusion = bf16[256,512]{1,0:T(8,128)(2,1)S(1)} fusion(bf16[128,512]{1,0:T(8,128)(2,1)S(1)} %collective-permute-done.2.refs_3_, bf16[64,512]{1,0:T(8,128)(2,1)S(1)} %collective-permute-done.1.refs_2_, bf16[32,512]{1,0:T(8,128)(2,1)S(1)} %collective-permute-done.refs_1_, bf16[32,512]{1,0:T(8,128)(2,1)} %bitcast.10), kind=kLoop, calls=%fused_computation.4 | loop fusion | flops 1048576 | bytes 524288 | tf_op jit(solution)/shard_map/concatenate | solution.py:76
  18.1 1.8 %collective-permute-start.3 = (bf16[256,512]{1,0:T(8,128)(2,1)S(1)}, bf16[256,512]{1,0:T(8,128)(2,1)S(1)}, u32[]{:S(2)}, u32[]{:S(2)}) collective-permute-start(bf16[256,512]{1,0:T(8,128)(2,1)S(1)} %pad_maximum_fusion), channel_id=1, source_target_pairs={{0,2},{2,0},{4,6},{6,4},{8,10},{10,8},{12,14},{14,12},{16,18},{18,... | collective-permute-start | bytes 786440 | tf_op jit(solution)/shard_map/ppermute | solution.py:13
  19.9 0.7 %broadcast_xor_fusion.away_ref = s32[16]{0:T(128)S(1)} fusion(s32[16]{0:T(128)} %constant.20.clone, s32[]{:T(128)S(6)} %axis_index.23), kind=kLoop, calls=%fused_computation.22 | loop fusion | flops 16 | bytes 132 | tf_op jit(solution)/shard_map/xor | solution.py:81
  20.5 4.0 %collective-permute-done.3.refs_4_ = bf16[256,512]{1,0:T(8,128)(2,1)S(1)} collective-permute-done((bf16[256,512]{1,0:T(8,128)(2,1)S(1)}, bf16[256,512]{1,0:T(8,128)(2,1)S(1)}, u32[]{:S(2)}, u32[]{:S(2)}) %collective-permute-start.3) | collective-permute-done | bytes 262176 | tf_op jit(solution)/shard_map/ppermute | solution.py:13
  24.5 0.0 collective-permute-start.8
  24.6 0.5 collective-permute-start.7
  25.1 1.3 %gather_fusion = s32[16]{0:T(128)S(1)} fusion(s32[16]{0:T(128)} %constant.20.clone, s32[1024]{0:T(1024)S(1)} %pad_clamp_fusion), kind=kCustom, calls=%fused_computation | custom fusion | bytes 192 | tf_op jit(solution)/shard_map/gather | solution.py:85
  26.4 0.1 collective-permute-start.5
  26.5 0.4 collective-permute-start.6
  26.9 0.1 pad_add_fusion.home_ref
  27.0 1.3 %dynamic_slice.3 = s32[1,1]{0,1:T(1,128)} dynamic-slice(s32[16,2]{0,1:T(2,128)} %param.11, s32[]{:T(128)S(6)} %select_n.17, s32[]{:T(128)S(6)} %select_n.18), dynamic_slice_sizes={1,1} | dynamic-slice | bytes 12 | tf_op jit(solution)/shard_map/dynamic_slice | solution.py:88
  28.3 0.0 collective-permute-done.4.refs_5_
  28.3 0.0 collective-permute-done.5.refs_6_
  28.3 0.0 collective-permute-done.6.refs_7_
  28.3 0.0 collective-permute-done.7.refs_8_
  28.3 0.0 collective-permute-done.8.refs_9_
  28.3 0.0 copy-start
  28.3 0.7 %copy-done = bf16[1,32,512]{2,1,0:T(8,128)(2,1)S(1)} copy-done((bf16[1,32,512]{2,1,0:T(8,128)(2,1)S(1)}, bf16[1,32,512]{2,1,0:T(8,128)(2,1)}, u32[]{:S(2)}) %copy-start) | copy-done | bytes 32792
  29.1 0.0 copy-start.1
  29.1 1.6 %copy-done.1 = bf16[4,512,512]{2,1,0:T(8,128)(2,1)S(1)} copy-done((bf16[4,512,512]{2,1,0:T(8,128)(2,1)S(1)}, bf16[4,512,512]{2,1,0:T(8,128)(2,1)}, u32[]{:S(2)}) %copy-start.1) | copy-done | bytes 2097176
  30.7 0.0 copy-start.2
  30.7 1.6 %copy-done.2 = bf16[4,512,512]{2,1,0:T(8,128)(2,1)S(1)} copy-done((bf16[4,512,512]{2,1,0:T(8,128)(2,1)S(1)}, bf16[4,512,512]{2,1,0:T(8,128)(2,1)}, u32[]{:S(2)}) %copy-start.2) | copy-done | bytes 2097176
  32.3 0.0 copy-start.3
  32.3 0.7 %copy-done.3 = s32[4]{0:T(128)S(1)} copy-done((s32[4]{0:T(128)S(1)}, s32[4]{0:T(128)}, u32[]{:S(2)}) %copy-start.3) | copy-done | bytes 40
  32.9 3.7 %shard_map.73 = (f32[256,512]{1,0:T(8,128)S(1)}, bf16[256,512]{1,0:T(8,128)(2,1)S(1)}) custom-call(s32[18]{0:T(128)S(1)} %pad_add_fusion.home_ref, s32[16]{0:T(128)S(1)} %broadcast_xor_fusion.away_ref, s32[4]{0:T(128)S(1)} %copy-done.3, s32[1]{0:T(128)} %bitcast.1.count_ref, bf16[32,512]{1,0:T(8,128)(2,1)S(1)} %bitcast.11, ...), custom_call_target="tpu_custom_call" | custom-call | flops 2147483648 | bytes 4194304 | tf_op jit(solution)/shard_map/pallas_call | solution.py:97
  36.6 1.8 %collective-permute-start.9 = (bf16[256,512]{1,0:T(8,128)(2,1)S(1)}, bf16[256,512]{1,0:T(8,128)(2,1)S(1)}, u32[]{:S(2)}, u32[]{:S(2)}) collective-permute-start(bf16[256,512]{1,0:T(8,128)(2,1)S(1)} %get-tuple-element.8), channel_id=1, source_target_pairs={{0,2},{2,0},{4,6},{6,4},{8,10},{10,8},{12,14},{14,12},{16,18},{18,... | collective-permute-start | bytes 786440 | tf_op jit(solution)/shard_map/ppermute | solution.py:13
  38.4 6.6 %collective-permute-done.9 = bf16[256,512]{1,0:T(8,128)(2,1)S(1)} collective-permute-done((bf16[256,512]{1,0:T(8,128)(2,1)S(1)}, bf16[256,512]{1,0:T(8,128)(2,1)S(1)}, u32[]{:S(2)}, u32[]{:S(2)}) %collective-permute-start.9) | collective-permute-done | bytes 262176 | tf_op jit(solution)/shard_map/ppermute | solution.py:13
  44.9 0.1 convert_element_type.24
  45.0 0.1 slice_add_fusion.1
  45.1 1.8 %collective-permute-start.10 = (bf16[128,512]{1,0:T(8,128)(2,1)S(1)}, bf16[128,512]{1,0:T(8,128)(2,1)S(1)}, u32[]{:S(2)}, u32[]{:S(2)}) collective-permute-start(bf16[128,512]{1,0:T(8,128)(2,1)S(1)} %get-tuple-element.10), channel_id=1, source_target_pairs={{0,4},{2,6},{4,0},{6,2},{8,12},{10,14},{12,8},{14,10},{16,20},{18,... | collective-permute-start | bytes 393224 | tf_op jit(solution)/shard_map/ppermute | solution.py:13
  46.9 3.2 %collective-permute-done.10 = bf16[128,512]{1,0:T(8,128)(2,1)S(1)} collective-permute-done((bf16[128,512]{1,0:T(8,128)(2,1)S(1)}, bf16[128,512]{1,0:T(8,128)(2,1)S(1)}, u32[]{:S(2)}, u32[]{:S(2)}) %collective-permute-start.10) | collective-permute-done | bytes 131104 | tf_op jit(solution)/shard_map/ppermute | solution.py:13
  50.2 1.6 %collective-permute-start.11 = (bf16[64,512]{1,0:T(8,128)(2,1)S(1)}, bf16[64,512]{1,0:T(8,128)(2,1)S(1)}, u32[]{:S(2)}, u32[]{:S(2)}) collective-permute-start(bf16[64,512]{1,0:T(8,128)(2,1)S(1)} %get-tuple-element.12), channel_id=1, source_target_pairs={{0,8},{2,10},{4,12},{6,14},{8,0},{10,2},{12,4},{14,6},{16,24},{18,... | collective-permute-start | bytes 196616 | tf_op jit(solution)/shard_map/ppermute | solution.py:13
  51.8 2.7 %collective-permute-done.11 = bf16[64,512]{1,0:T(8,128)(2,1)S(1)} collective-permute-done((bf16[64,512]{1,0:T(8,128)(2,1)S(1)}, bf16[64,512]{1,0:T(8,128)(2,1)S(1)}, u32[]{:S(2)}, u32[]{:S(2)}) %collective-permute-start.11) | collective-permute-done | bytes 65568 | tf_op jit(solution)/shard_map/ppermute | solution.py:13
  54.6 3.0 %collective-permute-start.12 = (bf16[32,512]{1,0:T(8,128)(2,1)S(1)}, bf16[32,512]{1,0:T(8,128)(2,1)S(1)}, u32[]{:S(2)}, u32[]{:S(2)}) collective-permute-start(bf16[32,512]{1,0:T(8,128)(2,1)S(1)} %fusion.2), channel_id=1, source_target_pairs={{0,16},{2,18},{4,20},{6,22},{8,24},{10,26},{12,28},{14,30},{16,0},... | collective-permute-start | bytes 98312 | tf_op jit(solution)/shard_map/ppermute | solution.py:13
  57.6 1.9 %collective-permute-done.12 = bf16[32,512]{1,0:T(8,128)(2,1)S(1)} collective-permute-done((bf16[32,512]{1,0:T(8,128)(2,1)S(1)}, bf16[32,512]{1,0:T(8,128)(2,1)S(1)}, u32[]{:S(2)}, u32[]{:S(2)}) %collective-permute-start.12) | collective-permute-done | bytes 32800 | tf_op jit(solution)/shard_map/ppermute | solution.py:13
  59.5 0.6 %fusion.6 = bf16[1,32,512]{2,1,0:T(8,128)(2,1)} fusion(bf16[32,512]{1,0:T(8,128)(2,1)S(1)} %collective-permute-done.12, f32[64,512]{1,0:T(8,128)S(1)} %convert_element_type.28, f32[64,512]{1,0:T(8,128)S(1)} %get-tuple-element.11), kind=kLoop, calls=%fused_computation.16 | loop fusion | flops 81920 | bytes 196608 | tf_op jit(solution)/shard_map/broadcast_in_dim | solution.py:124
  (7 shorter events, 0.1 us)
Async XLA Ops:
  0.0 6.5 %collective-permute-start = (bf16[32,512]{1,0:T(8,128)(2,1)}, bf16[32,512]{1,0:T(8,128)(2,1)S(1)}, u32[]{:S(2)}, u32[]{:S(2)}) collective-permute-start(bf16[32,512]{1,0:T(8,128)(2,1)} %bitcast.6), channel_id=1, source_target_pairs={{0,16},{2,18},{4,20},{6,22},{8,24},{10,26},{12,28},{14,30},{16,0},... | collective-permute-start | bytes 98312 | tf_op jit(solution)/shard_map/ppermute | solution.py:13
  7.3 4.3 %collective-permute-start.1 = (bf16[64,512]{1,0:T(8,128)(2,1)S(1)}, bf16[64,512]{1,0:T(8,128)(2,1)S(1)}, u32[]{:S(2)}, u32[]{:S(2)}) collective-permute-start(bf16[64,512]{1,0:T(8,128)(2,1)S(1)} %pad_maximum_fusion.2), channel_id=1, source_target_pairs={{0,8},{2,10},{4,12},{6,14},{8,0},{10,2},{12,4},{14,6},{16,24},{18,... | collective-permute-start | bytes 196616 | tf_op jit(solution)/shard_map/ppermute | solution.py:13
  12.3 5.0 %collective-permute-start.2 = (bf16[128,512]{1,0:T(8,128)(2,1)S(1)}, bf16[128,512]{1,0:T(8,128)(2,1)S(1)}, u32[]{:S(2)}, u32[]{:S(2)}) collective-permute-start(bf16[128,512]{1,0:T(8,128)(2,1)S(1)} %pad_maximum_fusion.1), channel_id=1, source_target_pairs={{0,4},{2,6},{4,0},{6,2},{8,12},{10,14},{12,8},{14,10},{16,20},{18,... | collective-permute-start | bytes 393224 | tf_op jit(solution)/shard_map/ppermute | solution.py:13
  14.1 14.2 %collective-permute-start.4 = (bf16[32,512]{1,0:T(8,128)(2,1)}, bf16[32,512]{1,0:T(8,128)(2,1)S(1)}, u32[]{:S(2)}, u32[]{:S(2)}) collective-permute-start(bf16[32,512]{1,0:T(8,128)(2,1)} %bitcast.9), channel_id=1, source_target_pairs={{0,1},{1,0},{2,3},{3,2},{4,5},{5,4},{6,7},{7,6},{8,9},{9,8},{10,11... | collective-permute-start | bytes 98312 | tf_op jit(solution)/shard_map/ppermute | solution.py:13
  18.1 6.4 %collective-permute-start.3 = (bf16[256,512]{1,0:T(8,128)(2,1)S(1)}, bf16[256,512]{1,0:T(8,128)(2,1)S(1)}, u32[]{:S(2)}, u32[]{:S(2)}) collective-permute-start(bf16[256,512]{1,0:T(8,128)(2,1)S(1)} %pad_maximum_fusion), channel_id=1, source_target_pairs={{0,2},{2,0},{4,6},{6,4},{8,10},{10,8},{12,14},{14,12},{16,18},{18,... | collective-permute-start | bytes 786440 | tf_op jit(solution)/shard_map/ppermute | solution.py:13
  24.5 3.8 %collective-permute-start.8 = (bf16[256,512]{1,0:T(8,128)(2,1)S(1)}, bf16[256,512]{1,0:T(8,128)(2,1)S(1)}, u32[]{:S(2)}, u32[]{:S(2)}) collective-permute-start(bf16[256,512]{1,0:T(8,128)(2,1)S(1)} %collective-permute-done.3.refs_4_), channel_id=1, source_target_pairs={{0,1},{1,0},{2,3},{3,2},{4,5},{5,4},{6,7},{7,6},{8,9},{9,8},{10,11... | collective-permute-start | bytes 786440 | tf_op jit(solution)/shard_map/ppermute | solution.py:13
  24.6 3.7 %collective-permute-start.7 = (bf16[128,512]{1,0:T(8,128)(2,1)S(1)}, bf16[128,512]{1,0:T(8,128)(2,1)S(1)}, u32[]{:S(2)}, u32[]{:S(2)}) collective-permute-start(bf16[128,512]{1,0:T(8,128)(2,1)S(1)} %collective-permute-done.2.refs_3_), channel_id=1, source_target_pairs={{0,1},{1,0},{2,3},{3,2},{4,5},{5,4},{6,7},{7,6},{8,9},{9,8},{10,11... | collective-permute-start | bytes 393224 | tf_op jit(solution)/shard_map/ppermute | solution.py:13
  26.4 1.9 %collective-permute-start.5 = (bf16[32,512]{1,0:T(8,128)(2,1)S(1)}, bf16[32,512]{1,0:T(8,128)(2,1)S(1)}, u32[]{:S(2)}, u32[]{:S(2)}) collective-permute-start(bf16[32,512]{1,0:T(8,128)(2,1)S(1)} %collective-permute-done.refs_1_), channel_id=1, source_target_pairs={{0,1},{1,0},{2,3},{3,2},{4,5},{5,4},{6,7},{7,6},{8,9},{9,8},{10,11... | collective-permute-start | bytes 98312 | tf_op jit(solution)/shard_map/ppermute | solution.py:13
  26.5 1.8 %collective-permute-start.6 = (bf16[64,512]{1,0:T(8,128)(2,1)S(1)}, bf16[64,512]{1,0:T(8,128)(2,1)S(1)}, u32[]{:S(2)}, u32[]{:S(2)}) collective-permute-start(bf16[64,512]{1,0:T(8,128)(2,1)S(1)} %collective-permute-done.1.refs_2_), channel_id=1, source_target_pairs={{0,1},{1,0},{2,3},{3,2},{4,5},{5,4},{6,7},{7,6},{8,9},{9,8},{10,11... | collective-permute-start | bytes 196616 | tf_op jit(solution)/shard_map/ppermute | solution.py:13
  28.3 0.8 %copy-start = (bf16[1,32,512]{2,1,0:T(8,128)(2,1)S(1)}, bf16[1,32,512]{2,1,0:T(8,128)(2,1)}, u32[]{:S(2)}) copy-start(bf16[1,32,512]{2,1,0:T(8,128)(2,1)} %param.7) | copy-start | bytes 98308
  29.1 1.6 %copy-start.1 = (bf16[4,512,512]{2,1,0:T(8,128)(2,1)S(1)}, bf16[4,512,512]{2,1,0:T(8,128)(2,1)}, u32[]{:S(2)}) copy-start(bf16[4,512,512]{2,1,0:T(8,128)(2,1)} %refs_10_.1) | copy-start | bytes 6291460
  30.7 1.6 %copy-start.2 = (bf16[4,512,512]{2,1,0:T(8,128)(2,1)S(1)}, bf16[4,512,512]{2,1,0:T(8,128)(2,1)}, u32[]{:S(2)}) copy-start(bf16[4,512,512]{2,1,0:T(8,128)(2,1)} %refs_11_.1) | copy-start | bytes 6291460
  32.3 0.7 %copy-start.3 = (s32[4]{0:T(128)S(1)}, s32[4]{0:T(128)}, u32[]{:S(2)}) copy-start(s32[4]{0:T(128)} %sector_ref.1) | copy-start | bytes 52
  36.6 8.4 %collective-permute-start.9 = (bf16[256,512]{1,0:T(8,128)(2,1)S(1)}, bf16[256,512]{1,0:T(8,128)(2,1)S(1)}, u32[]{:S(2)}, u32[]{:S(2)}) collective-permute-start(bf16[256,512]{1,0:T(8,128)(2,1)S(1)} %get-tuple-element.8), channel_id=1, source_target_pairs={{0,2},{2,0},{4,6},{6,4},{8,10},{10,8},{12,14},{14,12},{16,18},{18,... | collective-permute-start | bytes 786440 | tf_op jit(solution)/shard_map/ppermute | solution.py:13
  45.1 5.0 %collective-permute-start.10 = (bf16[128,512]{1,0:T(8,128)(2,1)S(1)}, bf16[128,512]{1,0:T(8,128)(2,1)S(1)}, u32[]{:S(2)}, u32[]{:S(2)}) collective-permute-start(bf16[128,512]{1,0:T(8,128)(2,1)S(1)} %get-tuple-element.10), channel_id=1, source_target_pairs={{0,4},{2,6},{4,0},{6,2},{8,12},{10,14},{12,8},{14,10},{16,20},{18,... | collective-permute-start | bytes 393224 | tf_op jit(solution)/shard_map/ppermute | solution.py:13
  50.2 4.3 %collective-permute-start.11 = (bf16[64,512]{1,0:T(8,128)(2,1)S(1)}, bf16[64,512]{1,0:T(8,128)(2,1)S(1)}, u32[]{:S(2)}, u32[]{:S(2)}) collective-permute-start(bf16[64,512]{1,0:T(8,128)(2,1)S(1)} %get-tuple-element.12), channel_id=1, source_target_pairs={{0,8},{2,10},{4,12},{6,14},{8,0},{10,2},{12,4},{14,6},{16,24},{18,... | collective-permute-start | bytes 196616 | tf_op jit(solution)/shard_map/ppermute | solution.py:13
  54.6 4.9 %collective-permute-start.12 = (bf16[32,512]{1,0:T(8,128)(2,1)S(1)}, bf16[32,512]{1,0:T(8,128)(2,1)S(1)}, u32[]{:S(2)}, u32[]{:S(2)}) collective-permute-start(bf16[32,512]{1,0:T(8,128)(2,1)S(1)} %fusion.2), channel_id=1, source_target_pairs={{0,16},{2,18},{4,20},{6,22},{8,24},{10,26},{12,28},{14,30},{16,0},... | collective-permute-start | bytes 98312 | tf_op jit(solution)/shard_map/ppermute | solution.py:13

commit v2 on v0

v2 whole, which is shorter than its diff:
```python
import functools

import jax
import jax.numpy as jnp
from jax import lax
from jax.experimental import pallas as pl
from jax.experimental.pallas import tpu as pltpu
from jax.sharding import PartitionSpec as P

F32, BF16 = jnp.float32, jnp.bfloat16
SMEM = pl.BlockSpec(memory_space=pltpu.SMEM)
VMEM = pl.BlockSpec(memory_space=pltpu.VMEM)
HBM = pl.BlockSpec(memory_space=pl.ANY)


def exchange(value, axis, mask):
    size = lax.axis_size(axis)
    return lax.ppermute(value, axis, [(i, i ^ mask) for i in range(size)])


def spread(position, masks):
    return sum(mask for bit, mask in enumerate(masks) if position >> bit & 1)


def load_kernel(*refs):
    count = len(refs) // 2
    sources, places, sems = refs[:count], refs[count : 2 * count], refs[2 * count]
    copies = [
        pltpu.make_async_copy(source, place, sems.at[i])
        for i, (source, place) in enumerate(zip(sources, places))
    ]
    for copy in copies:
        copy.start()
    for copy in copies:
        copy.wait()


def load(*arrays):
    size = sum(array.size * array.dtype.itemsize for array in arrays)
    return pl.pallas_call(
        load_kernel,
        out_shape=tuple(jax.ShapeDtypeStruct(a.shape, a.dtype) for a in arrays),
        in_specs=[HBM] * len(arrays),
        out_specs=(VMEM,) * len(arrays),
        scratch_shapes=[pltpu.SemaphoreType.DMA((len(arrays),))],
        compiler_params=pltpu.CompilerParams(vmem_limit_bytes=16 * 2**20),
        cost_estimate=pl.CostEstimate(flops=0, bytes_accessed=2 * size, transcendentals=0),
    )(*arrays)


def row_sums(distances, rows, place, count, sector_ref, left_ref, right_ref, wave_ref):
    starts = [pl.multiple_of((place ^ distance) * rows, rows) for distance in distances]
    total = None
    for slot in range(left_ref.shape[0]):
        left = jnp.concatenate([left_ref[slot, pl.ds(start, rows), :] for start in starts], axis=0)
        halfway = jnp.dot(left, wave_ref[sector_ref[slot]], preferred_element_type=F32).astype(BF16)
        halfway = jnp.where(slot < count, halfway, jnp.zeros_like(halfway))
        product = lax.dot_general(
            halfway, right_ref[slot], (((1,), (1,)), ((), ())), preferred_element_type=F32
        )
        total = product if total is None else total + product
    return total


def far_kernel(gathered, scattered, near, rows, sector_ref, counts_ref, *refs):
    pieces, (left_ref, right_ref, wave_ref, first_ref, second_ref) = refs[:-5], refs[-5:]
    place, sector = lax.axis_index("op"), lax.axis_index("sec")
    distances = [gather ^ quarter for quarter in (0, near[0], near[1], near[0] ^ near[1]) for gather in gathered]
    row = 0
    for ref in pieces:
        away, first = divmod(row, len(distances) * rows)
        for part in range(ref.shape[0] // rows):
            start = pl.multiple_of((place ^ distances[first // rows + part]) * rows, rows)
            wave_ref[sector ^ away, pl.ds(start, rows), :] = ref[part * rows : (part + 1) * rows, :]
        row += ref.shape[0]
    total = row_sums(
        [distance ^ near[0] ^ near[1] for distance in scattered],
        rows, place, counts_ref[place, sector], sector_ref, left_ref, right_ref, wave_ref,
    ).astype(BF16)
    half = first_ref.shape[0]
    first_ref[...], second_ref[...] = total[:half, :], total[half:, :]


def near_kernel(scattered, near, rows, sector_ref, counts_ref, left_ref, right_ref, wave_ref, *sums):
    place, sector = lax.axis_index("op"), lax.axis_index("sec")
    total = row_sums(
        [distance ^ quarter for quarter in (0, *near) for distance in scattered],
        rows, place, counts_ref[place, sector], sector_ref, left_ref, right_ref, wave_ref,
    )
    row = 0
    for ref in sums:
        ref[...] = total[row : row + ref.shape[0], :].astype(ref.dtype)
        row += ref.shape[0]


def by_neighbours(wavefunction, left_ops, right_ops, in_sector, counts):
    op_devices, sec_devices = lax.axis_size("op"), lax.axis_size("sec")
    slots, left_rows, order = left_ops.shape
    masks = [1 << bit for bit in range(op_devices.bit_length() - 1)]
    near, line = masks[:2], masks[2:]
    rows, wide = left_rows // op_devices, left_rows // 4
    gathered = [spread(p, line[::-1]) for p in range(op_devices // 4)]
    scattered = gathered
    barrier = lax.optimization_barrier

    def to_sectors(piece):
        return [exchange(piece, "sec", away) for away in range(1, sec_devices)]

    left, right, held = load(left_ops, right_ops, wavefunction[0])
    for step, mask in enumerate(line[::-1]):
        arrived = exchange(wavefunction[0] if step == 0 else held, "op", mask)
        held = jnp.concatenate([held, arrived], axis=0)
    half = held.shape[0] // 2
    beside = [exchange(held, "op", mask) for mask in near]
    others = [to_sectors(held)]
    beside, others = barrier((beside, others))
    diagonal = [exchange(beside[1][:half], "op", near[0]), exchange(beside[0][half:], "op", near[1])]
    others.append(to_sectors(jnp.concatenate(beside, axis=0)))
    diagonal, others = barrier((diagonal, others))
    others.append(to_sectors(jnp.concatenate(diagonal, axis=0)))
    pieces = [held, *beside, *diagonal]
    for away in range(sec_devices - 1):
        pieces += [group[away] for group in others]

    def cost(part):
        return pl.CostEstimate(
            flops=int(4 * slots * left_rows * order * order * part),
            bytes_accessed=int(4 * slots * left_rows * order),
            transcendentals=0,
        )

    params = pltpu.CompilerParams(vmem_limit_bytes=24 * 2**20)
    wave, *sends = pl.pallas_call(
        functools.partial(far_kernel, gathered, scattered, near, rows),
        out_shape=(
            jax.ShapeDtypeStruct((sec_devices, order, order), BF16),
            jax.ShapeDtypeStruct((wide // 2, order), BF16),
            jax.ShapeDtypeStruct((wide // 2, order), BF16),
        ),
        in_specs=[SMEM] * 2 + [VMEM] * (len(pieces) + 2),
        out_specs=(VMEM,) * 3,
        compiler_params=params,
        cost_estimate=cost(0.25),
    )(in_sector, counts, *pieces, left, right)

    passed = [exchange(send, "op", mask) for send, mask in zip(sends, near)]
    own, x_first, x_second, y_first, y_second = pl.pallas_call(
        functools.partial(near_kernel, scattered, near, rows),
        out_shape=(
            jax.ShapeDtypeStruct((wide, order), F32),
            jax.ShapeDtypeStruct((wide // 2, order), BF16),
            jax.ShapeDtypeStruct((wide // 2, order), F32),
            jax.ShapeDtypeStruct((wide // 2, order), F32),
            jax.ShapeDtypeStruct((wide // 2, order), BF16),
        ),
        in_specs=[SMEM] * 2 + [VMEM] * 3,
        out_specs=(VMEM,) * 5,
        compiler_params=params,
        cost_estimate=cost(0.75),
    )(in_sector, counts, left, right, wave)
    to_x = jnp.concatenate([x_first, (x_second + passed[1].astype(F32)).astype(BF16)], axis=0)
    to_y = jnp.concatenate([(y_first + passed[0].astype(F32)).astype(BF16), y_second], axis=0)
    keep = own + exchange(to_x, "op", near[0]).astype(F32) + exchange(to_y, "op", near[1]).astype(F32)
    for mask in line:
        half = keep.shape[0] // 2
        keep = keep[:half] + exchange(keep[half:].astype(BF16), "op", mask).astype(F32)
    factor = (op_devices * slots) ** (-0.5)
    return (keep * factor).astype(BF16)[None]


def by_collectives(wavefunction, left_ops, right_ops, in_sector, counts):
    slots, left_rows, order = left_ops.shape
    by_rows = lax.all_gather(wavefunction, "op", axis=1, tiled=True)
    gathered = lax.all_gather(by_rows, "sec", axis=0, tiled=True)

    def term(slot, summed):
        halfway = jnp.dot(left_ops[slot], gathered[in_sector[slot]], preferred_element_type=F32)
        product = lax.dot_general(
            halfway.astype(BF16), right_ops[slot], (((1,), (1,)), ((), ())), preferred_element_type=F32
        )
        return summed + product

    count = counts[lax.axis_index("op"), lax.axis_index("sec")]
    summed = lax.fori_loop(0, count, term, jnp.zeros((left_rows, order), F32))
    shares = lax.psum_scatter(summed, "op", scatter_dimension=0, tiled=True)
    factor = (lax.axis_size("op") * slots) ** (-0.5)
    return (shares * factor).astype(BF16)[None]


def shards(wavefunction, left_ops, right_ops, in_sector, counts):
    op_devices, sec_devices = lax.axis_size("op"), lax.axis_size("sec")
    powers = all(size & (size - 1) == 0 for size in (op_devices, sec_devices))
    tiles = left_ops.shape[1] % (16 * op_devices) == 0 and left_ops.shape[1] == left_ops.shape[2]
    body = by_neighbours if powers and tiles and op_devices >= 8 else by_collectives
    return body(wavefunction, left_ops, right_ops, in_sector, counts)


def solution(mesh):
    placed = (
        P("sec", "op", None),
        P(("op", "sec"), None, None),
        P(("op", "sec"), None, None),
        P(("op", "sec")),
        P(),
    )
    return jax.shard_map(
        shards, mesh=mesh, in_specs=placed, out_specs=P("sec", "op", None), check_vma=False
    )
```

time: 170 us -> 56.1 us (0.33)
  waiting for transfers between devices: 98.5 us -> 26.5 us
  blocking collectives: 48.2 us -> 0 us
  starting transfers between devices: 0.04 us -> 16.4 us
  between operations: 13.4 us -> 0.16 us
  Pallas kernels: 0 us -> 4.96 us
  local copies, waits for them, and re-layouts: 3.02 us -> 7 us
  loops' own time: 3.2 us -> 0 us
  matrix products: 2.1 us -> 0 us
    reduce_scatter x1 -> x0, waiting for transfers between devices: 94.8 us -> none  [shards(): shares = lax.psum_scatter(summed, 'op', scatter_dimension=0, tiled=True)]
    all_gather x1 -> x0, blocking collectives: 48.2 us -> none  [shards(): by_rows = lax.all_gather(wavefunction, 'op', axis=1, tiled=True)]
    ppermute x0 -> x15, waiting for transfers between devices: none -> 26.5 us  [exchange(): return lax.ppermute(value, axis, [(i, i ^ mask) for i in range(size)])]
    ppermute x0 -> x15, starting transfers between devices: none -> 16.4 us  [exchange(): return lax.ppermute(value, axis, [(i, i ^ mask) for i in range(size)])]
    unnamed x4 -> x17, local copies, waits for them, and re-layouts: 0.97 us -> 6.96 us
    pallas_call x0 -> x3, Pallas kernels: none -> 4.96 us  [the longest x1 2.59 us: by_neighbours(): pl.pallas_call(functools.partial(near_kernel, scattered, near, rows), out...]
    all_gather x1 -> x0, waiting for transfers between devices: 3.67 us -> none  [shards(): gathered = lax.all_gather(by_rows, 'sec', axis=0, tiled=True)]
    another operation x1 -> x0, loops' own time: 3.2 us -> none  [shards(): summed = lax.fori_loop(0, own_count, local_step, initial)]
  transfers between devices with their start and end apart: 2 -> 15, of which waited for: 2 -> 12; matrix products, arithmetic and copies ran while one was open for 1% -> 0% of each run, Pallas kernels for 0% -> 5%
where the time goes in v2:
time: 56.1 us; the launch traced here: 55.8 us
  waiting for transfers between devices  26.5 us (47%)
  starting transfers between devices  16.4 us (29%)
  local copies, waits for them, and re-layouts  7 us (12%)
  Pallas kernels  4.96 us (9%)
  other arithmetic  0.78 us (1%)
    ppermute x15, waiting for transfers between devices, exchange(): return lax.ppermute(value, axis, [(i, i ^ mask) for i in range(size)])  26.5 us
    ppermute x15, starting transfers between devices, exchange(): return lax.ppermute(value, axis, [(i, i ^ mask) for i in range(size)])  16.4 us
    unnamed x17, local copies, waits for them, and re-layouts  6.96 us
    pallas_call x1, Pallas kernels, by_neighbours(): pl.pallas_call(functools.partial(near_kernel, scattered, near, rows), out...  2.59 us
    pallas_call x1, Pallas kernels, by_neighbours(): pl.pallas_call(functools.partial(far_kernel, gathered, scattered, near, r...  2.03 us
  transfers between devices with their start and end apart: 15, of which 12 were waited for; matrix products, arithmetic and copies ran while one was open for 0% of the time, Pallas kernels for 5%

profile of v2, /device:TPU:0, one launch (start us, length us, event | category | flops | bytes accessed | tf_op | source)
XLA Modules:
  0.0 55.8 jit_solution(152063215841526751)
XLA Ops:
  0.0 4.0 %collective-permute-start = (bf16[32,512]{1,0:T(8,128)(2,1)}, bf16[32,512]{1,0:T(8,128)(2,1)S(1)}, u32[]{:S(2)}, u32[]{:S(2)}) collective-permute-start(bf16[32,512]{1,0:T(8,128)(2,1)} %bitcast.3), channel_id=1, source_target_pairs={{0,16},{2,18},{4,20},{6,22},{8,24},{10,26},{12,28},{14,30},{16,0},... | collective-permute-start | bytes 98312 | tf_op jit(solution)/shard_map/ppermute | solution.py:18
  4.0 0.0 copy-start
  4.0 1.6 %copy-done = bf16[4,512,512]{2,1,0:T(8,128)(2,1)S(1)} copy-done((bf16[4,512,512]{2,1,0:T(8,128)(2,1)S(1)}, bf16[4,512,512]{2,1,0:T(8,128)(2,1)}, u32[]{:S(2)}) %copy-start) | copy-done | bytes 2097176
  5.6 0.0 copy-start.1
  5.6 1.6 %copy-done.1 = bf16[4,512,512]{2,1,0:T(8,128)(2,1)S(1)} copy-done((bf16[4,512,512]{2,1,0:T(8,128)(2,1)S(1)}, bf16[4,512,512]{2,1,0:T(8,128)(2,1)}, u32[]{:S(2)}) %copy-start.1) | copy-done | bytes 2097176
  7.2 0.0 copy-start.4
  7.2 0.8 %copy-done.4 = bf16[1,32,512]{2,1,0:T(8,128)(2,1)S(1)} copy-done((bf16[1,32,512]{2,1,0:T(8,128)(2,1)S(1)}, bf16[1,32,512]{2,1,0:T(8,128)(2,1)}, u32[]{:S(2)}) %copy-start.4) | copy-done | bytes 32792
  8.0 0.0 copy-start.6
  8.0 0.0 copy-start.5
  8.0 0.3 shard_map.55
  8.3 0.0 copy-start.2
  8.3 1.3 %copy-done.2 = bf16[4,512,512]{2,1,0:T(8,128)(2,1)} copy-done((bf16[4,512,512]{2,1,0:T(8,128)(2,1)}, bf16[4,512,512]{2,1,0:T(8,128)(2,1)S(1)}, u32[]{:S(2)}) %copy-start.2) | copy-done | bytes 2097176
  9.7 0.0 collective-permute-done
  9.7 1.6 %collective-permute-start.1 = (bf16[64,512]{1,0:T(8,128)(2,1)S(1)}, bf16[64,512]{1,0:T(8,128)(2,1)S(1)}, u32[]{:S(2)}, u32[]{:S(2)}) collective-permute-start(bf16[64,512]{1,0:T(8,128)(2,1)S(1)} %pad_maximum_fusion.4), channel_id=1, source_target_pairs={{0,8},{2,10},{4,12},{6,14},{8,0},{10,2},{12,4},{14,6},{16,24},{18,... | collective-permute-start | bytes 196616 | tf_op jit(solution)/shard_map/ppermute | solution.py:18
  11.3 2.7 %collective-permute-done.1 = bf16[64,512]{1,0:T(8,128)(2,1)S(1)} collective-permute-done((bf16[64,512]{1,0:T(8,128)(2,1)S(1)}, bf16[64,512]{1,0:T(8,128)(2,1)S(1)}, u32[]{:S(2)}, u32[]{:S(2)}) %collective-permute-start.1) | collective-permute-done | bytes 65568 | tf_op jit(solution)/shard_map/ppermute | solution.py:18
  14.0 0.0 collective-permute-start.4
  14.0 1.6 %collective-permute-start.3 = (bf16[128,512]{1,0:T(8,128)(2,1)S(1)}, bf16[128,512]{1,0:T(8,128)(2,1)S(1)}, u32[]{:S(2)}, u32[]{:S(2)}) collective-permute-start(bf16[128,512]{1,0:T(8,128)(2,1)S(1)} %constant_dynamic-update-slice_fusion.refs_0_), channel_id=1, source_target_pairs={{0,4},{2,6},{4,0},{6,2},{8,12},{10,14},{12,8},{14,10},{16,20},{18,... | collective-permute-start | bytes 393224 | tf_op jit(solution)/shard_map/ppermute | solution.py:18
  15.6 1.5 %collective-permute-start.2 = (bf16[128,512]{1,0:T(8,128)(2,1)S(1)}, bf16[128,512]{1,0:T(8,128)(2,1)S(1)}, u32[]{:S(2)}, u32[]{:S(2)}) collective-permute-start(bf16[128,512]{1,0:T(8,128)(2,1)S(1)} %constant_dynamic-update-slice_fusion.refs_0_), channel_id=1, source_target_pairs={{0,2},{2,0},{4,6},{6,4},{8,10},{10,8},{12,14},{14,12},{16,18},{18,... | collective-permute-start | bytes 393224 | tf_op jit(solution)/shard_map/ppermute | solution.py:18
  17.1 0.0 collective-permute-done.4.refs_5_
  17.1 2.8 %collective-permute-done.3.refs_2_ = bf16[128,512]{1,0:T(8,128)(2,1)S(1)} collective-permute-done((bf16[128,512]{1,0:T(8,128)(2,1)S(1)}, bf16[128,512]{1,0:T(8,128)(2,1)S(1)}, u32[]{:S(2)}, u32[]{:S(2)}) %collective-permute-start.3) | collective-permute-done | bytes 131104 | tf_op jit(solution)/shard_map/ppermute | solution.py:18
  19.9 1.2 %collective-permute-done.2.refs_1_ = bf16[128,512]{1,0:T(8,128)(2,1)S(1)} collective-permute-done((bf16[128,512]{1,0:T(8,128)(2,1)S(1)}, bf16[128,512]{1,0:T(8,128)(2,1)S(1)}, u32[]{:S(2)}, u32[]{:S(2)}) %collective-permute-start.2) | collective-permute-done | bytes 131104 | tf_op jit(solution)/shard_map/ppermute | solution.py:18
  21.2 0.1 collective-permute-start.7
  21.3 1.6 %collective-permute-start.5 = (bf16[64,512]{1,0:T(8,128)(2,1)S(1)}, bf16[64,512]{1,0:T(8,128)(2,1)S(1)}, u32[]{:S(2)}, u32[]{:S(2)}) collective-permute-start(bf16[64,512]{1,0:T(8,128)(2,1)S(1)} %slice.20), channel_id=1, source_target_pairs={{0,2},{2,0},{4,6},{6,4},{8,10},{10,8},{12,14},{14,12},{16,18},{18,... | collective-permute-start | bytes 196616 | tf_op jit(solution)/shard_map/ppermute | solution.py:18
  22.9 0.5 collective-permute-start.6
  23.4 2.5 %collective-permute-done.5.refs_3_ = bf16[64,512]{1,0:T(8,128)(2,1)S(1)} collective-permute-done((bf16[64,512]{1,0:T(8,128)(2,1)S(1)}, bf16[64,512]{1,0:T(8,128)(2,1)S(1)}, u32[]{:S(2)}, u32[]{:S(2)}) %collective-permute-start.5) | collective-permute-done | bytes 65568 | tf_op jit(solution)/shard_map/ppermute | solution.py:18
  25.9 1.3 %collective-permute-done.6.refs_4_ = bf16[64,512]{1,0:T(8,128)(2,1)S(1)} collective-permute-done((bf16[64,512]{1,0:T(8,128)(2,1)S(1)}, bf16[64,512]{1,0:T(8,128)(2,1)S(1)}, u32[]{:S(2)}, u32[]{:S(2)}) %collective-permute-start.6) | collective-permute-done | bytes 65568 | tf_op jit(solution)/shard_map/ppermute | solution.py:18
  27.1 0.0 collective-permute-done.7.refs_6_
  27.2 0.1 collective-permute-start.8
  27.2 0.0 copy-done.6
  27.2 0.1 copy.7.counts_ref
  27.3 1.2 %collective-permute-done.8.refs_7_ = bf16[128,512]{1,0:T(8,128)(2,1)S(1)} collective-permute-done((bf16[128,512]{1,0:T(8,128)(2,1)S(1)}, bf16[128,512]{1,0:T(8,128)(2,1)S(1)}, u32[]{:S(2)}, u32[]{:S(2)}) %collective-permute-start.8) | collective-permute-done | bytes 131104 | tf_op jit(solution)/shard_map/ppermute | solution.py:18
  28.6 0.0 copy-done.5
  28.6 0.0 copy-start.3
  28.6 1.6 %copy-done.3 = bf16[4,512,512]{2,1,0:T(8,128)(2,1)S(1)} copy-done((bf16[4,512,512]{2,1,0:T(8,128)(2,1)S(1)}, bf16[4,512,512]{2,1,0:T(8,128)(2,1)}, u32[]{:S(2)}) %copy-start.3) | copy-done | bytes 2097176
  30.2 2.0 %shard_map.56 = (bf16[2,512,512]{2,1,0:T(8,128)(2,1)S(1)}, bf16[64,512]{1,0:T(8,128)(2,1)S(1)}, bf16[64,512]{1,0:T(8,128)(2,1)S(1)}) custom-call(s32[4]{0:T(128)S(1)} %copy-done.5, s32[16,2]{1,0:T(8,128)S(1)} %copy.7.counts_ref, bf16[128,512]{1,0:T(8,128)(2,1)S(1)} %constant_dynamic-update-slice_fusion.refs_0_, ...), custom_call_target="tpu_custom_call" | custom-call | flops 536870912 | bytes 4194304 | tf_op jit(solution)/shard_map/pallas_call | solution.py:133
  32.2 0.6 %collective-permute-start.11 = (bf16[64,512]{1,0:T(8,128)(2,1)S(1)}, bf16[64,512]{1,0:T(8,128)(2,1)S(1)}, u32[]{:S(2)}, u32[]{:S(2)}) collective-permute-start(bf16[64,512]{1,0:T(8,128)(2,1)S(1)} %get-tuple-element.39), channel_id=1, source_target_pairs={{0,2},{2,0},{4,6},{6,4},{8,10},{10,8},{12,14},{14,12},{16,18},{18,... | collective-permute-start | bytes 196616 | tf_op jit(solution)/shard_map/ppermute | solution.py:18
  32.8 2.6 %shard_map.57 = (f32[128,512]{1,0:T(8,128)S(1)}, bf16[64,512]{1,0:T(8,128)(2,1)S(1)}, f32[64,512]{1,0:T(8,128)S(1)}, f32[64,512]{1,0:T(8,128)S(1)}, bf16[64,512]{1,0:T(8,128)(2,1)S(1)}) custom-call(s32[4]{0:T(128)S(1)} %copy-done.5, s32[16,2]{1,0:T(8,128)S(1)} %copy.7.counts_ref, bf16[4,512,512]{2,1,0:T(8,128)(2,1)S(1)} %get-tuple-element.23.refs_8_.left_ref, ...), custom_call_target="tpu_custom_call" | custom-call | flops 1610612736 | bytes 4194304 | tf_op jit(solution)/shard_map/pallas_call | solution.py:147
  35.4 0.6 %collective-permute-start.9 = (bf16[64,512]{1,0:T(8,128)(2,1)S(1)}, bf16[64,512]{1,0:T(8,128)(2,1)S(1)}, u32[]{:S(2)}, u32[]{:S(2)}) collective-permute-start(bf16[64,512]{1,0:T(8,128)(2,1)S(1)} %get-tuple-element.37), channel_id=1, source_target_pairs={{0,4},{2,6},{4,0},{6,2},{8,12},{10,14},{12,8},{14,10},{16,20},{18,... | collective-permute-start | bytes 196616 | tf_op jit(solution)/shard_map/ppermute | solution.py:18
  36.0 0.6 %collective-permute-done.11 = bf16[64,512]{1,0:T(8,128)(2,1)S(1)} collective-permute-done((bf16[64,512]{1,0:T(8,128)(2,1)S(1)}, bf16[64,512]{1,0:T(8,128)(2,1)S(1)}, u32[]{:S(2)}, u32[]{:S(2)}) %collective-permute-start.11) | collective-permute-done | bytes 65568 | tf_op jit(solution)/shard_map/ppermute | solution.py:18
  36.6 1.0 %collective-permute-start.12 = (bf16[128,512]{1,0:T(8,128)(2,1)S(1)}, bf16[128,512]{1,0:T(8,128)(2,1)S(1)}, u32[]{:S(2)}, u32[]{:S(2)}) collective-permute-start(bf16[128,512]{1,0:T(8,128)(2,1)S(1)} %pad_maximum_fusion.3), channel_id=1, source_target_pairs={{0,4},{2,6},{4,0},{6,2},{8,12},{10,14},{12,8},{14,10},{16,20},{18,... | collective-permute-start | bytes 393224 | tf_op jit(solution)/shard_map/ppermute | solution.py:18
  37.6 2.8 %collective-permute-done.9 = bf16[64,512]{1,0:T(8,128)(2,1)S(1)} collective-permute-done((bf16[64,512]{1,0:T(8,128)(2,1)S(1)}, bf16[64,512]{1,0:T(8,128)(2,1)S(1)}, u32[]{:S(2)}, u32[]{:S(2)}) %collective-permute-start.9) | collective-permute-done | bytes 65568 | tf_op jit(solution)/shard_map/ppermute | solution.py:18
  40.5 1.6 %collective-permute-start.10 = (bf16[128,512]{1,0:T(8,128)(2,1)S(1)}, bf16[128,512]{1,0:T(8,128)(2,1)S(1)}, u32[]{:S(2)}, u32[]{:S(2)}) collective-permute-start(bf16[128,512]{1,0:T(8,128)(2,1)S(1)} %pad_maximum_fusion.2), channel_id=1, source_target_pairs={{0,2},{2,0},{4,6},{6,4},{8,10},{10,8},{12,14},{14,12},{16,18},{18,... | collective-permute-start | bytes 393224 | tf_op jit(solution)/shard_map/ppermute | solution.py:18
  42.0 0.1 collective-permute-done.12
  42.1 3.4 %collective-permute-done.10 = bf16[128,512]{1,0:T(8,128)(2,1)S(1)} collective-permute-done((bf16[128,512]{1,0:T(8,128)(2,1)S(1)}, bf16[128,512]{1,0:T(8,128)(2,1)S(1)}, u32[]{:S(2)}, u32[]{:S(2)}) %collective-permute-start.10) | collective-permute-done | bytes 131104 | tf_op jit(solution)/shard_map/ppermute | solution.py:18
  45.6 1.6 %collective-permute-start.13 = (bf16[64,512]{1,0:T(8,128)(2,1)S(1)}, bf16[64,512]{1,0:T(8,128)(2,1)S(1)}, u32[]{:S(2)}, u32[]{:S(2)}) collective-permute-start(bf16[64,512]{1,0:T(8,128)(2,1)S(1)} %slice.40), channel_id=1, source_target_pairs={{0,8},{2,10},{4,12},{6,14},{8,0},{10,2},{12,4},{14,6},{16,24},{18,... | collective-permute-start | bytes 196616 | tf_op jit(solution)/shard_map/ppermute | solution.py:18
  47.2 3.0 %collective-permute-done.13 = bf16[64,512]{1,0:T(8,128)(2,1)S(1)} collective-permute-done((bf16[64,512]{1,0:T(8,128)(2,1)S(1)}, bf16[64,512]{1,0:T(8,128)(2,1)S(1)}, u32[]{:S(2)}, u32[]{:S(2)}) %collective-permute-start.13) | collective-permute-done | bytes 65568 | tf_op jit(solution)/shard_map/ppermute | solution.py:18
  50.3 0.1 collective-permute-start.14
  50.4 4.8 %collective-permute-done.14 = bf16[32,512]{1,0:T(8,128)(2,1)S(1)} collective-permute-done((bf16[32,512]{1,0:T(8,128)(2,1)S(1)}, bf16[32,512]{1,0:T(8,128)(2,1)S(1)}, u32[]{:S(2)}, u32[]{:S(2)}) %collective-permute-start.14) | collective-permute-done | bytes 32800 | tf_op jit(solution)/shard_map/ppermute | solution.py:18
  55.2 0.6 %fusion.2 = bf16[1,32,512]{2,1,0:T(8,128)(2,1)} fusion(bf16[32,512]{1,0:T(8,128)(2,1)S(1)} %collective-permute-done.14, f32[64,512]{1,0:T(8,128)S(1)} %slice_add_fusion), kind=kLoop, calls=%fused_computation.14 | loop fusion | flops 65536 | bytes 131072 | tf_op jit(solution)/shard_map/broadcast_in_dim | solution.py:168
  (16 shorter events, 0.2 us)
Async XLA Ops:
  0.0 9.7 %collective-permute-start = (bf16[32,512]{1,0:T(8,128)(2,1)}, bf16[32,512]{1,0:T(8,128)(2,1)S(1)}, u32[]{:S(2)}, u32[]{:S(2)}) collective-permute-start(bf16[32,512]{1,0:T(8,128)(2,1)} %bitcast.3), channel_id=1, source_target_pairs={{0,16},{2,18},{4,20},{6,22},{8,24},{10,26},{12,28},{14,30},{16,0},... | collective-permute-start | bytes 98312 | tf_op jit(solution)/shard_map/ppermute | solution.py:18
  4.0 1.6 %copy-start = (bf16[4,512,512]{2,1,0:T(8,128)(2,1)S(1)}, bf16[4,512,512]{2,1,0:T(8,128)(2,1)}, u32[]{:S(2)}) copy-start(bf16[4,512,512]{2,1,0:T(8,128)(2,1)} %refs_0_.1) | copy-start | bytes 6291460
  5.6 1.6 %copy-start.1 = (bf16[4,512,512]{2,1,0:T(8,128)(2,1)S(1)}, bf16[4,512,512]{2,1,0:T(8,128)(2,1)}, u32[]{:S(2)}) copy-start(bf16[4,512,512]{2,1,0:T(8,128)(2,1)} %refs_1_.1) | copy-start | bytes 6291460
  7.2 0.8 %copy-start.4 = (bf16[1,32,512]{2,1,0:T(8,128)(2,1)S(1)}, bf16[1,32,512]{2,1,0:T(8,128)(2,1)}, u32[]{:S(2)}) copy-start(bf16[1,32,512]{2,1,0:T(8,128)(2,1)} %param.5) | copy-start | bytes 98308
  8.0 19.3 %copy-start.6 = (s32[16,2]{0,1:T(2,128)S(1)}, s32[16,2]{0,1:T(2,128)}, u32[]{:S(2)}) copy-start(s32[16,2]{0,1:T(2,128)} %param.9) | copy-start | bytes 388
  8.0 20.6 %copy-start.5 = (s32[4]{0:T(128)S(1)}, s32[4]{0:T(128)}, u32[]{:S(2)}) copy-start(s32[4]{0:T(128)} %sector_ref.3) | copy-start | bytes 52
  8.3 1.3 %copy-start.2 = (bf16[4,512,512]{2,1,0:T(8,128)(2,1)}, bf16[4,512,512]{2,1,0:T(8,128)(2,1)S(1)}, u32[]{:S(2)}) copy-start(bf16[4,512,512]{2,1,0:T(8,128)(2,1)S(1)} %get-tuple-element.24.refs_9_.right_ref) | copy-start | bytes 6291460
  9.7 4.3 %collective-permute-start.1 = (bf16[64,512]{1,0:T(8,128)(2,1)S(1)}, bf16[64,512]{1,0:T(8,128)(2,1)S(1)}, u32[]{:S(2)}, u32[]{:S(2)}) collective-permute-start(bf16[64,512]{1,0:T(8,128)(2,1)S(1)} %pad_maximum_fusion.4), channel_id=1, source_target_pairs={{0,8},{2,10},{4,12},{6,14},{8,0},{10,2},{12,4},{14,6},{16,24},{18,... | collective-permute-start | bytes 196616 | tf_op jit(solution)/shard_map/ppermute | solution.py:18
  14.0 3.1 %collective-permute-start.4 = (bf16[128,512]{1,0:T(8,128)(2,1)S(1)}, bf16[128,512]{1,0:T(8,128)(2,1)S(1)}, u32[]{:S(2)}, u32[]{:S(2)}) collective-permute-start(bf16[128,512]{1,0:T(8,128)(2,1)S(1)} %constant_dynamic-update-slice_fusion.refs_0_), channel_id=1, source_target_pairs={{0,1},{1,0},{2,3},{3,2},{4,5},{5,4},{6,7},{7,6},{8,9},{9,8},{10,11... | collective-permute-start | bytes 393224 | tf_op jit(solution)/shard_map/ppermute | solution.py:18
  14.0 5.9 %collective-permute-start.3 = (bf16[128,512]{1,0:T(8,128)(2,1)S(1)}, bf16[128,512]{1,0:T(8,128)(2,1)S(1)}, u32[]{:S(2)}, u32[]{:S(2)}) collective-permute-start(bf16[128,512]{1,0:T(8,128)(2,1)S(1)} %constant_dynamic-update-slice_fusion.refs_0_), channel_id=1, source_target_pairs={{0,4},{2,6},{4,0},{6,2},{8,12},{10,14},{12,8},{14,10},{16,20},{18,... | collective-permute-start | bytes 393224 | tf_op jit(solution)/shard_map/ppermute | solution.py:18
  15.6 5.6 %collective-permute-start.2 = (bf16[128,512]{1,0:T(8,128)(2,1)S(1)}, bf16[128,512]{1,0:T(8,128)(2,1)S(1)}, u32[]{:S(2)}, u32[]{:S(2)}) collective-permute-start(bf16[128,512]{1,0:T(8,128)(2,1)S(1)} %constant_dynamic-update-slice_fusion.refs_0_), channel_id=1, source_target_pairs={{0,2},{2,0},{4,6},{6,4},{8,10},{10,8},{12,14},{14,12},{16,18},{18,... | collective-permute-start | bytes 393224 | tf_op jit(solution)/shard_map/ppermute | solution.py:18
  21.2 5.9 %collective-permute-start.7 = (bf16[256,512]{1,0:T(8,128)(2,1)S(1)}, bf16[256,512]{1,0:T(8,128)(2,1)S(1)}, u32[]{:S(2)}, u32[]{:S(2)}) collective-permute-start(bf16[256,512]{1,0:T(8,128)(2,1)S(1)} %pad_maximum_fusion), channel_id=1, source_target_pairs={{0,1},{1,0},{2,3},{3,2},{4,5},{5,4},{6,7},{7,6},{8,9},{9,8},{10,11... | collective-permute-start | bytes 786440 | tf_op jit(solution)/shard_map/ppermute | solution.py:18
  21.3 4.5 %collective-permute-start.5 = (bf16[64,512]{1,0:T(8,128)(2,1)S(1)}, bf16[64,512]{1,0:T(8,128)(2,1)S(1)}, u32[]{:S(2)}, u32[]{:S(2)}) collective-permute-start(bf16[64,512]{1,0:T(8,128)(2,1)S(1)} %slice.20), channel_id=1, source_target_pairs={{0,2},{2,0},{4,6},{6,4},{8,10},{10,8},{12,14},{14,12},{16,18},{18,... | collective-permute-start | bytes 196616 | tf_op jit(solution)/shard_map/ppermute | solution.py:18
  22.9 4.3 %collective-permute-start.6 = (bf16[64,512]{1,0:T(8,128)(2,1)S(1)}, bf16[64,512]{1,0:T(8,128)(2,1)S(1)}, u32[]{:S(2)}, u32[]{:S(2)}) collective-permute-start(bf16[64,512]{1,0:T(8,128)(2,1)S(1)} %slice.21), channel_id=1, source_target_pairs={{0,4},{2,6},{4,0},{6,2},{8,12},{10,14},{12,8},{14,10},{16,20},{18,... | collective-permute-start | bytes 196616 | tf_op jit(solution)/shard_map/ppermute | solution.py:18
  27.2 1.4 %collective-permute-start.8 = (bf16[128,512]{1,0:T(8,128)(2,1)S(1)}, bf16[128,512]{1,0:T(8,128)(2,1)S(1)}, u32[]{:S(2)}, u32[]{:S(2)}) collective-permute-start(bf16[128,512]{1,0:T(8,128)(2,1)S(1)} %pad_maximum_fusion.1), channel_id=1, source_target_pairs={{0,1},{1,0},{2,3},{3,2},{4,5},{5,4},{6,7},{7,6},{8,9},{9,8},{10,11... | collective-permute-start | bytes 393224 | tf_op jit(solution)/shard_map/ppermute | solution.py:18
  28.6 1.6 %copy-start.3 = (bf16[4,512,512]{2,1,0:T(8,128)(2,1)S(1)}, bf16[4,512,512]{2,1,0:T(8,128)(2,1)}, u32[]{:S(2)}) copy-start(bf16[4,512,512]{2,1,0:T(8,128)(2,1)} %copy-done.2) | copy-start | bytes 6291460
  32.2 4.3 %collective-permute-start.11 = (bf16[64,512]{1,0:T(8,128)(2,1)S(1)}, bf16[64,512]{1,0:T(8,128)(2,1)S(1)}, u32[]{:S(2)}, u32[]{:S(2)}) collective-permute-start(bf16[64,512]{1,0:T(8,128)(2,1)S(1)} %get-tuple-element.39), channel_id=1, source_target_pairs={{0,2},{2,0},{4,6},{6,4},{8,10},{10,8},{12,14},{14,12},{16,18},{18,... | collective-permute-start | bytes 196616 | tf_op jit(solution)/shard_map/ppermute | solution.py:18
  35.4 5.0 %collective-permute-start.9 = (bf16[64,512]{1,0:T(8,128)(2,1)S(1)}, bf16[64,512]{1,0:T(8,128)(2,1)S(1)}, u32[]{:S(2)}, u32[]{:S(2)}) collective-permute-start(bf16[64,512]{1,0:T(8,128)(2,1)S(1)} %get-tuple-element.37), channel_id=1, source_target_pairs={{0,4},{2,6},{4,0},{6,2},{8,12},{10,14},{12,8},{14,10},{16,20},{18,... | collective-permute-start | bytes 196616 | tf_op jit(solution)/shard_map/ppermute | solution.py:18
  36.6 5.6 %collective-permute-start.12 = (bf16[128,512]{1,0:T(8,128)(2,1)S(1)}, bf16[128,512]{1,0:T(8,128)(2,1)S(1)}, u32[]{:S(2)}, u32[]{:S(2)}) collective-permute-start(bf16[128,512]{1,0:T(8,128)(2,1)S(1)} %pad_maximum_fusion.3), channel_id=1, source_target_pairs={{0,4},{2,6},{4,0},{6,2},{8,12},{10,14},{12,8},{14,10},{16,20},{18,... | collective-permute-start | bytes 393224 | tf_op jit(solution)/shard_map/ppermute | solution.py:18
  40.5 5.0 %collective-permute-start.10 = (bf16[128,512]{1,0:T(8,128)(2,1)S(1)}, bf16[128,512]{1,0:T(8,128)(2,1)S(1)}, u32[]{:S(2)}, u32[]{:S(2)}) collective-permute-start(bf16[128,512]{1,0:T(8,128)(2,1)S(1)} %pad_maximum_fusion.2), channel_id=1, source_target_pairs={{0,2},{2,0},{4,6},{6,4},{8,10},{10,8},{12,14},{14,12},{16,18},{18,... | collective-permute-start | bytes 393224 | tf_op jit(solution)/shard_map/ppermute | solution.py:18
  45.6 4.7 %collective-permute-start.13 = (bf16[64,512]{1,0:T(8,128)(2,1)S(1)}, bf16[64,512]{1,0:T(8,128)(2,1)S(1)}, u32[]{:S(2)}, u32[]{:S(2)}) collective-permute-start(bf16[64,512]{1,0:T(8,128)(2,1)S(1)} %slice.40), channel_id=1, source_target_pairs={{0,8},{2,10},{4,12},{6,14},{8,0},{10,2},{12,4},{14,6},{16,24},{18,... | collective-permute-start | bytes 196616 | tf_op jit(solution)/shard_map/ppermute | solution.py:18
  50.3 4.9 %collective-permute-start.14 = (bf16[32,512]{1,0:T(8,128)(2,1)S(1)}, bf16[32,512]{1,0:T(8,128)(2,1)S(1)}, u32[]{:S(2)}, u32[]{:S(2)}) collective-permute-start(bf16[32,512]{1,0:T(8,128)(2,1)S(1)} %slice.41), channel_id=1, source_target_pairs={{0,16},{2,18},{4,20},{6,22},{8,24},{10,26},{12,28},{14,30},{16,0},... | collective-permute-start | bytes 98312 | tf_op jit(solution)/shard_map/ppermute | solution.py:18

commit v3 on v0

v3 whole, which is shorter than its diff:
```python
import functools

import jax
import jax.numpy as jnp
from jax import lax
from jax.experimental import pallas as pl
from jax.experimental.pallas import tpu as pltpu
from jax.sharding import PartitionSpec as P

F32, BF16 = jnp.float32, jnp.bfloat16
SMEM = pl.BlockSpec(memory_space=pltpu.SMEM)
VMEM = pl.BlockSpec(memory_space=pltpu.VMEM)
HBM = pl.BlockSpec(memory_space=pltpu.HBM)


def exchange(value, axis, mask):
    size = lax.axis_size(axis)
    return lax.ppermute(value, axis, [(i, i ^ mask) for i in range(size)])


def spread(position, masks):
    return sum(mask for bit, mask in enumerate(masks) if position >> bit & 1)


def load_kernel(source, place, sem):
    copy = pltpu.make_async_copy(source, place, sem)
    copy.start()
    copy.wait()


def load(array):
    size = array.size * array.dtype.itemsize
    return pl.pallas_call(
        load_kernel,
        out_shape=jax.ShapeDtypeStruct(array.shape, array.dtype),
        in_specs=[HBM],
        out_specs=VMEM,
        scratch_shapes=[pltpu.SemaphoreType.DMA],
        compiler_params=pltpu.CompilerParams(vmem_limit_bytes=2**20),
        cost_estimate=pl.CostEstimate(flops=0, bytes_accessed=2 * size, transcendentals=0),
    )(array)


def terms_kernel(order, sector_ref, counts_ref, left_hbm, right_hbm, *refs):
    waves, (sum_ref, wave, left_ref, right_ref, left_sem, right_sem) = refs[:-6], refs[-6:]
    slots, rows = left_ref.shape[0], left_ref.shape[1] // len(order)
    lefts = [pltpu.make_async_copy(left_hbm.at[t], left_ref.at[t], left_sem.at[t]) for t in range(slots)]
    rights = [pltpu.make_async_copy(right_hbm.at[t], right_ref.at[t], right_sem.at[t]) for t in range(slots)]
    for left, right in zip(lefts, rights):
        left.start()
        right.start()
    for away, ref in enumerate(waves):
        for place, block in enumerate(order):
            group, part = divmod(place * rows, ref.shape[1])
            wave[away, block * rows : (block + 1) * rows, :] = ref[group, part : part + rows, :]
    sector = lax.axis_index("sec")
    count = counts_ref[lax.axis_index("op"), sector]
    total = None
    for slot in range(slots):
        away = lax.rem(sector - sector_ref[slot] + len(waves), len(waves))
        lefts[slot].wait()
        halfway = jnp.dot(left_ref[slot], wave[away], preferred_element_type=F32).astype(BF16)
        halfway = jnp.where(slot < count, halfway, jnp.zeros_like(halfway))
        rights[slot].wait()
        product = lax.dot_general(
            halfway, right_ref[slot], (((1,), (1,)), ((), ())), preferred_element_type=F32
        )
        total = product if total is None else total + product
    for place, block in enumerate(order):
        group, part = divmod(place * rows, sum_ref.shape[1])
        sum_ref[group, part : part + rows, :] = total[block * rows : (block + 1) * rows, :].astype(BF16)


def shards(wavefunction, left_ops, right_ops, in_sector, counts):
    op_devices, sec_devices = lax.axis_size("op"), lax.axis_size("sec")
    op_place = lax.axis_index("op")
    slots, left_rows, order = left_ops.shape
    near = min(8, op_devices) if op_devices & (op_devices - 1) == 0 else op_devices
    far = [near << bit for bit in range((op_devices // near).bit_length() - 1)]
    groups = [[far_place * near + i for i in range(near)] for far_place in range(op_devices // near)]
    blocks = [i + spread(p, far[::-1]) for i in range(near) for p in range(op_devices // near)]

    held = wavefunction[0]
    for step, mask in enumerate(far[::-1]):
        arrived = exchange(held, "op", mask)
        if step == 0:
            held = load(held)
        there = (op_place & mask) != 0
        held = jnp.concatenate(
            [jnp.where(there, arrived, held), jnp.where(there, held, arrived)], axis=0
        )
    held = jnp.broadcast_to(held[None], (near, *held.shape))
    gathered = [lax.all_to_all(held, "op", 0, 0, axis_index_groups=groups)]
    for away in range(1, sec_devices):
        turn = [(i, (i + away) % sec_devices) for i in range(sec_devices)]
        gathered.append(lax.ppermute(gathered[0], "sec", turn))

    summed = pl.pallas_call(
        functools.partial(terms_kernel, blocks),
        out_shape=jax.ShapeDtypeStruct((near, left_rows // near, order), BF16),
        in_specs=[SMEM] * 2 + [HBM] * 2 + [VMEM] * sec_devices,
        out_specs=VMEM,
        scratch_shapes=[
            pltpu.VMEM((sec_devices, order, order), BF16),
            pltpu.VMEM(left_ops.shape, BF16),
            pltpu.VMEM(right_ops.shape, BF16),
            pltpu.SemaphoreType.DMA((slots,)),
            pltpu.SemaphoreType.DMA((slots,)),
        ],
        compiler_params=pltpu.CompilerParams(vmem_limit_bytes=51 * 2**20),
        cost_estimate=pl.CostEstimate(
            flops=4 * slots * left_rows * order * order,
            bytes_accessed=4 * slots * left_rows * order,
            transcendentals=0,
        ),
    )(in_sector, counts, left_ops, right_ops, *gathered)

    parts = lax.all_to_all(summed, "op", 0, 0, axis_index_groups=groups)
    keep = jnp.sum(parts.astype(F32), axis=0)
    for mask in far:
        half = keep.shape[0] // 2
        there = (op_place & mask) != 0
        send = jnp.where(there, keep[:half], keep[half:]).astype(BF16)
        keep = jnp.where(there, keep[half:], keep[:half]) + exchange(send, "op", mask).astype(F32)
    factor = (op_devices * slots) ** (-0.5)
    return (keep * factor).astype(BF16)[None]


def solution(mesh):
    placed = (
        P("sec", "op", None),
        P(("op", "sec"), None, None),
        P(("op", "sec"), None, None),
        P(("op", "sec")),
        P(),
    )
    return jax.shard_map(
        shards, mesh=mesh, in_specs=placed, out_specs=P("sec", "op", None), check_vma=False
    )
```

time: 170 us -> 45.3 us (0.27)
  waiting for transfers between devices: 98.5 us -> 4.79 us
  blocking collectives: 48.2 us -> 25.2 us
  between operations: 13.4 us -> 0.06 us
  starting transfers between devices: 0.04 us -> 6.91 us
  Pallas kernels: 0 us -> 5.04 us
  loops' own time: 3.2 us -> 0 us
  matrix products: 2.1 us -> 0 us
    reduce_scatter x1 -> x0, waiting for transfers between devices: 94.8 us -> none  [shards(): shares = lax.psum_scatter(summed, 'op', scatter_dimension=0, tiled=True)]
    all_gather x1 -> x0, blocking collectives: 48.2 us -> none  [shards(): by_rows = lax.all_gather(wavefunction, 'op', axis=1, tiled=True)]
    all_to_all x0 -> x2, blocking collectives: none -> 25.2 us  [the longest x1 12.8 us: shards(): gathered = [lax.all_to_all(held, 'op', 0, 0, axis_index_groups=groups)]]
    ppermute x0 -> x3, starting transfers between devices: none -> 6.91 us  [the longest x2 6.91 us: exchange(): return lax.ppermute(value, axis, [(i, i ^ mask) for i in range(size)])]
    pallas_call x0 -> x2, Pallas kernels: none -> 5.04 us  [the longest x1 5.02 us: shards(): pl.pallas_call(functools.partial(terms_kernel, blocks), out_shape=jax.Sha...]
    ppermute x0 -> x3, waiting for transfers between devices: none -> 4.79 us  [the longest x2 3.64 us: exchange(): return lax.ppermute(value, axis, [(i, i ^ mask) for i in range(size)])]
    all_gather x1 -> x0, waiting for transfers between devices: 3.67 us -> none  [shards(): gathered = lax.all_gather(by_rows, 'sec', axis=0, tiled=True)]
    another operation x1 -> x0, loops' own time: 3.2 us -> none  [shards(): summed = lax.fori_loop(0, own_count, local_step, initial)]
  transfers between devices with their start and end apart: 2 -> 3, of which waited for: 2 -> 3; matrix products, arithmetic and copies ran while one was open for 1% -> 2% of each run, Pallas kernels for 0% -> 0%
where the time goes in v3:
time: 45.3 us; the launch traced here: 45 us
  blocking collectives  25.2 us (56%)
  starting transfers between devices  6.91 us (15%)
  Pallas kernels  5.04 us (11%)
  waiting for transfers between devices  4.79 us (11%)
  local copies, waits for them, and re-layouts  2.24 us (5%)
  other arithmetic  0.73 us (2%)
    all_to_all x1, blocking collectives, shards(): gathered = [lax.all_to_all(held, 'op', 0, 0, axis_index_groups=groups)]  12.8 us
    all_to_all x1, blocking collectives, shards(): parts = lax.all_to_all(summed, 'op', 0, 0, axis_index_groups=groups)  12.4 us
    ppermute x2, starting transfers between devices, exchange(): return lax.ppermute(value, axis, [(i, i ^ mask) for i in range(size)])  6.91 us
    pallas_call x1, Pallas kernels, shards(): pl.pallas_call(functools.partial(terms_kernel, blocks), out_shape=jax.Sha...  5.02 us
    ppermute x2, waiting for transfers between devices, exchange(): return lax.ppermute(value, axis, [(i, i ^ mask) for i in range(size)])  3.64 us
    unnamed x5, local copies, waits for them, and re-layouts  2.2 us
    ppermute x1, waiting for transfers between devices, shards(): gathered.append(lax.ppermute(gathered[0], 'sec', turn))  1.15 us
  transfers between devices with their start and end apart: 3, of which 3 were waited for; matrix products, arithmetic and copies ran while one was open for 2% of the time, Pallas kernels for 0%

profile of v3, /device:TPU:0, one launch (start us, length us, event | category | flops | bytes accessed | tf_op | source)
XLA Modules:
  0.0 45.0 jit_solution(3150960755401338362)
XLA Ops:
  0.0 4.0 %collective-permute-start = (bf16[32,512]{1,0:T(8,128)(2,1)}, bf16[32,512]{1,0:T(8,128)(2,1)S(1)}, u32[]{:S(2)}, u32[]{:S(2)}) collective-permute-start(bf16[32,512]{1,0:T(8,128)(2,1)} %bitcast.3), channel_id=1, source_target_pairs={{0,16},{2,18},{4,20},{6,22},{8,24},{10,26},{12,28},{14,30},{16,0},... | collective-permute-start | bytes 98312 | tf_op jit(solution)/shard_map/ppermute | solution.py:18
  4.0 0.0 copy-start
  4.0 0.8 %copy-done = bf16[1,32,512]{2,1,0:T(8,128)(2,1)S(1)} copy-done((bf16[1,32,512]{2,1,0:T(8,128)(2,1)S(1)}, bf16[1,32,512]{2,1,0:T(8,128)(2,1)}, u32[]{:S(2)}) %copy-start) | copy-done | bytes 32792
  4.9 1.6 %collective-permute-done = bf16[32,512]{1,0:T(8,128)(2,1)S(1)} collective-permute-done((bf16[32,512]{1,0:T(8,128)(2,1)}, bf16[32,512]{1,0:T(8,128)(2,1)S(1)}, u32[]{:S(2)}, u32[]{:S(2)}) %collective-permute-start) | collective-permute-done | bytes 32800 | tf_op jit(solution)/shard_map/ppermute | solution.py:18
  6.6 12.8 %all_to_all.10.refs_0_ = bf16[8,64,512]{2,1,0:T(8,128)(2,1)S(1)} all-to-all(bf16[8,64,512]{2,1,0:T(8,128)(2,1)S(1)} %broadcast_in_dim.4), channel_id=1, replica_groups={{0,2,4,6,8,10,12,14},{16,18,20,22,24,26,28,30},{1,3,5,7,9,11,13,15},{17..., dimensions={0} | all-to-all | bytes 1048576 | tf_op jit(solution)/shard_map/all_to_all | solution.py:93
  19.4 0.0 collective-permute-start.1
  19.4 0.8 %copy.6.counts_ref = s32[16,2]{1,0:T(8,128)S(1)} copy(s32[16,2]{0,1:T(2,128)} %param.9) | data formatting | bytes 256 | tf_op args[4]
  20.1 1.2 %collective-permute-done.1.refs_1_ = bf16[8,64,512]{2,1,0:T(8,128)(2,1)S(1)} collective-permute-done((bf16[8,64,512]{2,1,0:T(8,128)(2,1)S(1)}, bf16[8,64,512]{2,1,0:T(8,128)(2,1)S(1)}, u32[]{:S(2)}, u32[]{:S(2)}) %collective-permute-start.1) | collective-permute-done | bytes 524320 | tf_op jit(solution)/shard_map/ppermute | solution.py:96
  21.3 0.0 copy-start.1
  21.3 0.7 %copy-done.1 = s32[4]{0:T(128)S(1)} copy-done((s32[4]{0:T(128)S(1)}, s32[4]{0:T(128)}, u32[]{:S(2)}) %copy-start.1) | copy-done | bytes 40
  21.9 5.0 %shard_map.56 = bf16[8,64,512]{2,1,0:T(8,128)(2,1)S(1)} custom-call(s32[4]{0:T(128)S(1)} %copy-done.1, s32[16,2]{1,0:T(8,128)S(1)} %copy.6.counts_ref, bf16[4,512,512]{2,1,0:T(8,128)(2,1)} %left_hbm.1, bf16[4,512,512]{2,1,0:T(8,128)(2,1)} %right_hbm.1, bf16[8,64,512]{2,1,0:T(8,128)(2,1)S(1)} %all_to_all.10.refs_0_, ...), custom_call_target="tpu_custom_call" | custom-call | flops 2147483648 | bytes 4194304 | tf_op jit(solution)/shard_map/pallas_call | solution.py:98
  27.0 12.4 %all_to_all.11 = bf16[8,64,512]{2,1,0:T(8,128)(2,1)S(1)} all-to-all(bf16[8,64,512]{2,1,0:T(8,128)(2,1)S(1)} %shard_map.56), channel_id=1, replica_groups={{0,2,4,6,8,10,12,14},{16,18,20,22,24,26,28,30},{1,3,5,7,9,11,13,15},{17..., dimensions={0} | all-to-all | bytes 1048576 | tf_op jit(solution)/shard_map/all_to_all | solution.py:118
  39.4 0.1 convert_reduce_fusion
  39.5 2.9 %collective-permute-start.2 = (bf16[32,512]{1,0:T(8,128)(2,1)S(1)}, bf16[32,512]{1,0:T(8,128)(2,1)S(1)}, u32[]{:S(2)}, u32[]{:S(2)}) collective-permute-start(bf16[32,512]{1,0:T(8,128)(2,1)S(1)} %select_convert_fusion), channel_id=1, source_target_pairs={{0,16},{2,18},{4,20},{6,22},{8,24},{10,26},{12,28},{14,30},{16,0},... | collective-permute-start | bytes 98312 | tf_op jit(solution)/shard_map/ppermute | solution.py:18
  42.3 2.0 %collective-permute-done.2 = bf16[32,512]{1,0:T(8,128)(2,1)S(1)} collective-permute-done((bf16[32,512]{1,0:T(8,128)(2,1)S(1)}, bf16[32,512]{1,0:T(8,128)(2,1)S(1)}, u32[]{:S(2)}, u32[]{:S(2)}) %collective-permute-start.2) | collective-permute-done | bytes 32800 | tf_op jit(solution)/shard_map/ppermute | solution.py:18
  44.4 0.6 %fusion = bf16[1,32,512]{2,1,0:T(8,128)(2,1)} fusion(bf16[32,512]{1,0:T(8,128)(2,1)S(1)} %collective-permute-done.2, f32[64,512]{1,0:T(8,128)S(1)} %convert_reduce_fusion, pred[]{:T(512)S(6)} %ne.4), kind=kLoop, calls=%fused_computation.4 | loop fusion | flops 81920 | bytes 196609 | tf_op jit(solution)/shard_map/broadcast_in_dim | solution.py:126
  (5 shorter events, 0.1 us)
Async XLA Ops:
  0.0 6.5 %collective-permute-start = (bf16[32,512]{1,0:T(8,128)(2,1)}, bf16[32,512]{1,0:T(8,128)(2,1)S(1)}, u32[]{:S(2)}, u32[]{:S(2)}) collective-permute-start(bf16[32,512]{1,0:T(8,128)(2,1)} %bitcast.3), channel_id=1, source_target_pairs={{0,16},{2,18},{4,20},{6,22},{8,24},{10,26},{12,28},{14,30},{16,0},... | collective-permute-start | bytes 98312 | tf_op jit(solution)/shard_map/ppermute | solution.py:18
  4.0 0.8 %copy-start = (bf16[1,32,512]{2,1,0:T(8,128)(2,1)S(1)}, bf16[1,32,512]{2,1,0:T(8,128)(2,1)}, u32[]{:S(2)}) copy-start(bf16[1,32,512]{2,1,0:T(8,128)(2,1)} %param.5) | copy-start | bytes 98308
  19.4 1.9 %collective-permute-start.1 = (bf16[8,64,512]{2,1,0:T(8,128)(2,1)S(1)}, bf16[8,64,512]{2,1,0:T(8,128)(2,1)S(1)}, u32[]{:S(2)}, u32[]{:S(2)}) collective-permute-start(bf16[8,64,512]{2,1,0:T(8,128)(2,1)S(1)} %all_to_all.10.refs_0_), channel_id=1, source_target_pairs={{0,1},{1,0},{2,3},{3,2},{4,5},{5,4},{6,7},{7,6},{8,9},{9,8},{10,11... | collective-permute-start | bytes 1572872 | tf_op jit(solution)/shard_map/ppermute | solution.py:96
  21.3 0.7 %copy-start.1 = (s32[4]{0:T(128)S(1)}, s32[4]{0:T(128)}, u32[]{:S(2)}) copy-start(s32[4]{0:T(128)} %sector_ref.1) | copy-start | bytes 52
  39.5 4.9 %collective-permute-start.2 = (bf16[32,512]{1,0:T(8,128)(2,1)S(1)}, bf16[32,512]{1,0:T(8,128)(2,1)S(1)}, u32[]{:S(2)}, u32[]{:S(2)}) collective-permute-start(bf16[32,512]{1,0:T(8,128)(2,1)S(1)} %select_convert_fusion), channel_id=1, source_target_pairs={{0,16},{2,18},{4,20},{6,22},{8,24},{10,26},{12,28},{14,30},{16,0},... | collective-permute-start | bytes 98312 | tf_op jit(solution)/shard_map/ppermute | solution.py:18

commit v4 on v3

v4 whole, which is shorter than its diff:
```python
import functools

import jax
import jax.numpy as jnp
from jax import lax
from jax.experimental import pallas as pl
from jax.experimental.pallas import tpu as pltpu
from jax.sharding import PartitionSpec as P

F32, BF16 = jnp.float32, jnp.bfloat16
SMEM = pl.BlockSpec(memory_space=pltpu.SMEM)
VMEM = pl.BlockSpec(memory_space=pltpu.VMEM)
HBM = pl.BlockSpec(memory_space=pltpu.HBM)


def exchange(value, axis, mask):
    size = lax.axis_size(axis)
    return lax.ppermute(value, axis, [(i, i ^ mask) for i in range(size)])


def spread(position, masks):
    return sum(mask for bit, mask in enumerate(masks) if position >> bit & 1)


def costs(bytes_accessed, flops=0):
    return pl.CostEstimate(flops=flops, bytes_accessed=bytes_accessed, transcendentals=0)


def load_kernel(source, place, sem):
    copy = pltpu.make_async_copy(source, place, sem)
    copy.start()
    copy.wait()


def load(array):
    return pl.pallas_call(
        load_kernel,
        out_shape=jax.ShapeDtypeStruct(array.shape, array.dtype),
        in_specs=[HBM],
        out_specs=VMEM,
        scratch_shapes=[pltpu.SemaphoreType.DMA],
        compiler_params=pltpu.CompilerParams(vmem_limit_bytes=2**20),
        cost_estimate=costs(2 * array.size * array.dtype.itemsize),
    )(array)


def in_order(order, rows, source, place):
    for position, block in enumerate(order):
        group, part = divmod(position * rows, source.shape[1])
        place[block * rows : (block + 1) * rows, :] = source[group, part : part + rows, :]


def scalars_kernel(sectors, sector_ref, counts_ref, scalars_ref):
    sector = lax.axis_index("sec")
    count = counts_ref[sector, lax.axis_index("op")]
    for slot in range(scalars_ref.shape[0]):
        away = lax.rem(sector - sector_ref[slot] + sectors, sectors)
        scalars_ref[slot] = jnp.where(slot < count, away, -1)


def terms_kernel(order, scalars_ref, left_ref, right_hbm, own_ref, *refs):
    others, (sum_ref, wave, right_ref, sems) = refs[:-4], refs[-4:]
    slots, rows = left_ref.shape[0], left_ref.shape[1] // len(order)
    copies = [pltpu.make_async_copy(right_hbm.at[t], right_ref.at[t], sems.at[t]) for t in range(slots)]
    for copy in copies:
        copy.start()
    wave[0] = own_ref[...]
    for away, ref in enumerate(others):
        in_order(order, rows, ref, wave.at[away + 1])
    halfways = []
    for slot in range(slots):
        away = scalars_ref[slot]
        halfway = jnp.dot(left_ref[slot], wave[jnp.maximum(away, 0)], preferred_element_type=F32).astype(BF16)
        halfways.append(jnp.where(away >= 0, halfway, jnp.zeros_like(halfway)))
    total = None
    for slot in range(slots):
        copies[slot].wait()
        product = lax.dot_general(
            halfways[slot], right_ref[slot], (((1,), (1,)), ((), ())), preferred_element_type=F32
        )
        total = product if total is None else total + product
    for place, block in enumerate(order):
        group, part = divmod(place * rows, sum_ref.shape[1])
        sum_ref[group, part : part + rows, :] = total[block * rows : (block + 1) * rows, :].astype(BF16)


def shards(wavefunction, left_ops, right_ops, in_sector, counts):
    op_devices, sec_devices = lax.axis_size("op"), lax.axis_size("sec")
    op_place = lax.axis_index("op")
    slots, left_rows, order = left_ops.shape
    near = min(8, op_devices) if op_devices & (op_devices - 1) == 0 else op_devices
    far = [near << bit for bit in range((op_devices // near).bit_length() - 1)]
    groups = [[far_place * near + i for i in range(near)] for far_place in range(op_devices // near)]
    blocks = [i + spread(p, far[::-1]) for i in range(near) for p in range(op_devices // near)]

    scalars = pl.pallas_call(
        functools.partial(scalars_kernel, sec_devices),
        out_shape=jax.ShapeDtypeStruct((slots,), jnp.int32),
        in_specs=[SMEM] * 2,
        out_specs=SMEM,
        compiler_params=pltpu.CompilerParams(vmem_limit_bytes=2**20),
    )(in_sector, counts.T)
    held = wavefunction[0]
    for step, mask in enumerate(far[::-1]):
        arrived = exchange(held, "op", mask)
        if step == 0:
            held, scalars = lax.optimization_barrier((load(held), scalars))
        there = (op_place & mask) != 0
        held = jnp.concatenate(
            [jnp.where(there, arrived, held), jnp.where(there, held, arrived)], axis=0
        )
    held = jnp.broadcast_to(held[None], (near, *held.shape))
    gathered = [lax.all_to_all(held, "op", 0, 0, axis_index_groups=groups)]
    for away in range(1, sec_devices):
        turn = [(i, (i + away) % sec_devices) for i in range(sec_devices)]
        gathered.append(lax.ppermute(gathered[0], "sec", turn))
    own = pl.pallas_call(
        functools.partial(in_order, blocks, left_rows // op_devices),
        out_shape=jax.ShapeDtypeStruct((order, order), BF16),
        in_specs=[VMEM],
        out_specs=VMEM,
        compiler_params=pltpu.CompilerParams(vmem_limit_bytes=2**20),
        cost_estimate=costs(4 * slots * left_rows * order),
    )(gathered[0])

    summed = pl.pallas_call(
        functools.partial(terms_kernel, blocks),
        out_shape=jax.ShapeDtypeStruct((near, left_rows // near, order), BF16),
        in_specs=[SMEM, VMEM, HBM] + [VMEM] * sec_devices,
        out_specs=VMEM,
        scratch_shapes=[
            pltpu.VMEM((sec_devices, order, order), BF16),
            pltpu.VMEM(right_ops.shape, BF16),
            pltpu.SemaphoreType.DMA((slots,)),
        ],
        compiler_params=pltpu.CompilerParams(vmem_limit_bytes=49 * 2**20),
        cost_estimate=costs(4 * slots * left_rows * order, 4 * slots * left_rows * order * order),
    )(scalars, left_ops, right_ops, own, *gathered[1:])

    parts = lax.all_to_all(summed, "op", 0, 0, axis_index_groups=groups)
    keep = jnp.sum(parts.astype(F32), axis=0)
    for mask in far:
        half = keep.shape[0] // 2
        there = (op_place & mask) != 0
        send = jnp.where(there, keep[:half], keep[half:]).astype(BF16)
        keep = jnp.where(there, keep[half:], keep[:half]) + exchange(send, "op", mask).astype(F32)
    factor = (op_devices * slots) ** (-0.5)
    return (keep * factor).astype(BF16)[None]


def solution(mesh):
    placed = (
        P("sec", "op", None),
        P(("op", "sec"), None, None),
        P(("op", "sec"), None, None),
        P(("op", "sec")),
        P(),
    )
    return jax.shard_map(
        shards, mesh=mesh, in_specs=placed, out_specs=P("sec", "op", None), check_vma=False
    )
```

time: 45.3 us -> 45.8 us (1.011)
  starting transfers between devices: 6.91 us -> 5.14 us
  blocking collectives: 25.2 us -> 26.1 us
  waiting for transfers between devices: 4.79 us -> 5.66 us
  Pallas kernels: 5.04 us -> 5.64 us
    ppermute x2, starting transfers between devices: 6.91 us -> 5.14 us  [exchange(): return lax.ppermute(value, axis, [(i, i ^ mask) for i in range(size)])]
    pallas_call x0 -> x2, Pallas kernels: none -> 1.2 us  [the longest x1 1.17 us: shards(): pl.pallas_call(functools.partial(scalars_kernel, sec_devices), out_shape=...]
    all_to_all x1, blocking collectives: 12.8 us -> 13.7 us  [shards(): gathered = [lax.all_to_all(held, 'op', 0, 0, axis_index_groups=groups)]]
    ppermute x1, waiting for transfers between devices: 1.15 us -> 1.87 us  [shards(): gathered.append(lax.ppermute(gathered[0], 'sec', turn))]
    pallas_call x1, Pallas kernels: 5.02 us -> 4.42 us  [shards(): pl.pallas_call(functools.partial(terms_kernel, blocks), out_shape=jax.Sha...]
    unnamed x5 -> x8, local copies, waits for them, and re-layouts: 2.2 us -> 2.12 us
  transfers between devices with their start and end apart: 3 -> 3, of which waited for: 3 -> 2; matrix products, arithmetic and copies ran while one was open for 2% -> 0% of each run, Pallas kernels for 0% -> 3%
where the time goes in v4:
time: 45.8 us; the launch traced here: 45.5 us
  blocking collectives  26.1 us (57%)
  waiting for transfers between devices  5.66 us (12%)
  Pallas kernels  5.64 us (12%)
  starting transfers between devices  5.14 us (11%)
  local copies, waits for them, and re-layouts  2.16 us (5%)
  other arithmetic  0.73 us (2%)
    all_to_all x1, blocking collectives, shards(): gathered = [lax.all_to_all(held, 'op', 0, 0, axis_index_groups=groups)]  13.7 us
    all_to_all x1, blocking collectives, shards(): parts = lax.all_to_all(summed, 'op', 0, 0, axis_index_groups=groups)  12.4 us
    ppermute x2, starting transfers between devices, exchange(): return lax.ppermute(value, axis, [(i, i ^ mask) for i in range(size)])  5.14 us
    pallas_call x1, Pallas kernels, shards(): pl.pallas_call(functools.partial(terms_kernel, blocks), out_shape=jax.Sha...  4.42 us
    ppermute x2, waiting for transfers between devices, exchange(): return lax.ppermute(value, axis, [(i, i ^ mask) for i in range(size)])  3.79 us
    unnamed x8, local copies, waits for them, and re-layouts  2.12 us
    ppermute x1, waiting for transfers between devices, shards(): gathered.append(lax.ppermute(gathered[0], 'sec', turn))  1.87 us
    pallas_call x1, Pallas kernels, shards(): pl.pallas_call(functools.partial(scalars_kernel, sec_devices), out_shape=...  1.17 us
  transfers between devices with their start and end apart: 3, of which 2 were waited for; matrix products, arithmetic and copies ran while one was open for 0% of the time, Pallas kernels for 3%

profile of v4, /device:TPU:0, one launch (start us, length us, event | category | flops | bytes accessed | tf_op | source)
XLA Modules:
  0.0 45.5 jit_solution(2327126274388737918)
XLA Ops:
  0.0 4.0 %collective-permute-start = (bf16[32,512]{1,0:T(8,128)(2,1)}, bf16[32,512]{1,0:T(8,128)(2,1)S(1)}, u32[]{:S(2)}, u32[]{:S(2)}) collective-permute-start(bf16[32,512]{1,0:T(8,128)(2,1)} %bitcast.4), channel_id=1, source_target_pairs={{0,16},{2,18},{4,20},{6,22},{8,24},{10,26},{12,28},{14,30},{16,0},... | collective-permute-start | bytes 98312 | tf_op jit(solution)/shard_map/ppermute | solution.py:18
  4.0 0.0 copy-start
  4.0 0.8 %copy-done = bf16[1,32,512]{2,1,0:T(8,128)(2,1)S(1)} copy-done((bf16[1,32,512]{2,1,0:T(8,128)(2,1)S(1)}, bf16[1,32,512]{2,1,0:T(8,128)(2,1)}, u32[]{:S(2)}) %copy-start) | copy-done | bytes 32792
  4.9 0.0 copy-start.1
  4.9 0.7 %copy-done.1 = s32[16,2]{0,1:T(2,128)S(1)} copy-done((s32[16,2]{0,1:T(2,128)S(1)}, s32[16,2]{0,1:T(2,128)}, u32[]{:S(2)}) %copy-start.1) | copy-done | bytes 152
  5.5 0.0 copy-start.2
  5.5 0.7 %copy-done.2 = s32[4]{0:T(128)S(1)} copy-done((s32[4]{0:T(128)S(1)}, s32[4]{0:T(128)}, u32[]{:S(2)}) %copy-start.2) | copy-done | bytes 40
  6.2 0.0 copy-start.3
  6.2 1.2 %shard_map.56.scalars_ref = s32[4]{0:T(128)S(1)} custom-call(s32[4]{0:T(128)S(1)} %copy-done.2, s32[2,16]{1,0:T(2,128)S(1)} %bitcast.6), custom_call_target="tpu_custom_call" | custom-call | tf_op jit(solution)/shard_map/pallas_call | solution.py:96
  7.4 0.0 collective-permute-done
  7.5 13.7 %all_to_all.10.source = bf16[8,64,512]{2,1,0:T(8,128)(2,1)S(1)} all-to-all(bf16[8,64,512]{2,1,0:T(8,128)(2,1)S(1)} %broadcast_in_dim.4), channel_id=1, replica_groups={{0,2,4,6,8,10,12,14},{16,18,20,22,24,26,28,30},{1,3,5,7,9,11,13,15},{17..., dimensions={0} | all-to-all | bytes 1048576 | tf_op jit(solution)/shard_map/all_to_all | solution.py:113
  21.1 0.0 collective-permute-start.1
  21.2 1.9 %collective-permute-done.1.refs_0_ = bf16[8,64,512]{2,1,0:T(8,128)(2,1)S(1)} collective-permute-done((bf16[8,64,512]{2,1,0:T(8,128)(2,1)S(1)}, bf16[8,64,512]{2,1,0:T(8,128)(2,1)S(1)}, u32[]{:S(2)}, u32[]{:S(2)}) %collective-permute-start.1) | collective-permute-done | bytes 524320 | tf_op jit(solution)/shard_map/ppermute | solution.py:116
  23.1 0.0 copy-done.3
  23.1 4.4 %shard_map.58 = bf16[8,64,512]{2,1,0:T(8,128)(2,1)S(1)} custom-call(s32[4]{0:T(128)S(1)} %shard_map.56.scalars_ref, bf16[4,512,512]{2,1,0:T(8,128)(2,1)S(1)} %copy-done.3, bf16[4,512,512]{2,1,0:T(8,128)(2,1)} %right_hbm.1, bf16[512,512]{1,0:T(8,128)(2,1)S(1)} %shard_map.57.own_ref, bf16[8,64,512]{2,1,0:T(8,128)(2,1)S(1)} %collective-permute-done.1.refs_0_), custom_call_target="tpu_custom_call" | custom-call | flops 2147483648 | bytes 4194304 | tf_op jit(solution)/shard_map/pallas_call | solution.py:126
  27.5 12.4 %all_to_all.11 = bf16[8,64,512]{2,1,0:T(8,128)(2,1)S(1)} all-to-all(bf16[8,64,512]{2,1,0:T(8,128)(2,1)S(1)} %shard_map.58), channel_id=1, replica_groups={{0,2,4,6,8,10,12,14},{16,18,20,22,24,26,28,30},{1,3,5,7,9,11,13,15},{17..., dimensions={0} | all-to-all | bytes 1048576 | tf_op jit(solution)/shard_map/all_to_all | solution.py:140
  39.9 0.1 convert_reduce_fusion
  40.0 1.1 %collective-permute-start.2 = (bf16[32,512]{1,0:T(8,128)(2,1)S(1)}, bf16[32,512]{1,0:T(8,128)(2,1)S(1)}, u32[]{:S(2)}, u32[]{:S(2)}) collective-permute-start(bf16[32,512]{1,0:T(8,128)(2,1)S(1)} %select_convert_fusion), channel_id=1, source_target_pairs={{0,16},{2,18},{4,20},{6,22},{8,24},{10,26},{12,28},{14,30},{16,0},... | collective-permute-start | bytes 98312 | tf_op jit(solution)/shard_map/ppermute | solution.py:18
  41.1 3.8 %collective-permute-done.2 = bf16[32,512]{1,0:T(8,128)(2,1)S(1)} collective-permute-done((bf16[32,512]{1,0:T(8,128)(2,1)S(1)}, bf16[32,512]{1,0:T(8,128)(2,1)S(1)}, u32[]{:S(2)}, u32[]{:S(2)}) %collective-permute-start.2) | collective-permute-done | bytes 32800 | tf_op jit(solution)/shard_map/ppermute | solution.py:18
  44.9 0.6 %fusion = bf16[1,32,512]{2,1,0:T(8,128)(2,1)} fusion(bf16[32,512]{1,0:T(8,128)(2,1)S(1)} %collective-permute-done.2, f32[64,512]{1,0:T(8,128)S(1)} %convert_reduce_fusion, pred[]{:T(512)S(6)} %ne.4), kind=kLoop, calls=%fused_computation.4 | loop fusion | flops 81920 | bytes 196609 | tf_op jit(solution)/shard_map/broadcast_in_dim | solution.py:148
  (6 shorter events, 0.1 us)
Async XLA Ops:
  0.0 7.4 %collective-permute-start = (bf16[32,512]{1,0:T(8,128)(2,1)}, bf16[32,512]{1,0:T(8,128)(2,1)S(1)}, u32[]{:S(2)}, u32[]{:S(2)}) collective-permute-start(bf16[32,512]{1,0:T(8,128)(2,1)} %bitcast.4), channel_id=1, source_target_pairs={{0,16},{2,18},{4,20},{6,22},{8,24},{10,26},{12,28},{14,30},{16,0},... | collective-permute-start | bytes 98312 | tf_op jit(solution)/shard_map/ppermute | solution.py:18
  4.0 0.8 %copy-start = (bf16[1,32,512]{2,1,0:T(8,128)(2,1)S(1)}, bf16[1,32,512]{2,1,0:T(8,128)(2,1)}, u32[]{:S(2)}) copy-start(bf16[1,32,512]{2,1,0:T(8,128)(2,1)} %param.5) | copy-start | bytes 98308
  4.9 0.7 %copy-start.1 = (s32[16,2]{0,1:T(2,128)S(1)}, s32[16,2]{0,1:T(2,128)}, u32[]{:S(2)}) copy-start(s32[16,2]{0,1:T(2,128)} %param.9) | copy-start | bytes 388
  5.5 0.7 %copy-start.2 = (s32[4]{0:T(128)S(1)}, s32[4]{0:T(128)}, u32[]{:S(2)}) copy-start(s32[4]{0:T(128)} %sector_ref.1) | copy-start | bytes 52
  6.2 16.9 %copy-start.3 = (bf16[4,512,512]{2,1,0:T(8,128)(2,1)S(1)}, bf16[4,512,512]{2,1,0:T(8,128)(2,1)}, u32[]{:S(2)}) copy-start(bf16[4,512,512]{2,1,0:T(8,128)(2,1)} %left_ref.1) | copy-start | bytes 6291460
  21.1 1.9 %collective-permute-start.1 = (bf16[8,64,512]{2,1,0:T(8,128)(2,1)S(1)}, bf16[8,64,512]{2,1,0:T(8,128)(2,1)S(1)}, u32[]{:S(2)}, u32[]{:S(2)}) collective-permute-start(bf16[8,64,512]{2,1,0:T(8,128)(2,1)S(1)} %all_to_all.10.source), channel_id=1, source_target_pairs={{0,1},{1,0},{2,3},{3,2},{4,5},{5,4},{6,7},{7,6},{8,9},{9,8},{10,11... | collective-permute-start | bytes 1572872 | tf_op jit(solution)/shard_map/ppermute | solution.py:116
  40.0 4.9 %collective-permute-start.2 = (bf16[32,512]{1,0:T(8,128)(2,1)S(1)}, bf16[32,512]{1,0:T(8,128)(2,1)S(1)}, u32[]{:S(2)}, u32[]{:S(2)}) collective-permute-start(bf16[32,512]{1,0:T(8,128)(2,1)S(1)} %select_convert_fusion), channel_id=1, source_target_pairs={{0,16},{2,18},{4,20},{6,22},{8,24},{10,26},{12,28},{14,30},{16,0},... | collective-permute-start | bytes 98312 | tf_op jit(solution)/shard_map/ppermute | solution.py:18

commit v5 on v4

--- a/solution.py
+++ b/solution.py
@@ -50,33 +50,29 @@
         place[block * rows : (block + 1) * rows, :] = source[group, part : part + rows, :]
 
 
-def scalars_kernel(sectors, sector_ref, counts_ref, scalars_ref):
-    sector = lax.axis_index("sec")
-    count = counts_ref[sector, lax.axis_index("op")]
-    for slot in range(scalars_ref.shape[0]):
-        away = lax.rem(sector - sector_ref[slot] + sectors, sectors)
-        scalars_ref[slot] = jnp.where(slot < count, away, -1)
-
-
-def terms_kernel(order, scalars_ref, left_ref, right_hbm, own_ref, *refs):
+def terms_kernel(order, sector_ref, counts_ref, left_ref, right_hbm, own_ref, *refs):
     others, (sum_ref, wave, right_ref, sems) = refs[:-4], refs[-4:]
-    slots, rows = left_ref.shape[0], left_ref.shape[1] // len(order)
+    slots, rows, sectors = left_ref.shape[0], left_ref.shape[1] // len(order), wave.shape[0]
     copies = [pltpu.make_async_copy(right_hbm.at[t], right_ref.at[t], sems.at[t]) for t in range(slots)]
     for copy in copies:
         copy.start()
     wave[0] = own_ref[...]
     for away, ref in enumerate(others):
         in_order(order, rows, ref, wave.at[away + 1])
-    halfways = []
+    sector = lax.axis_index("sec")
+    count = counts_ref[sector, lax.axis_index("op")]
+
+    def halfway(slot):
+        away = lax.rem(sector - sector_ref[slot] + sectors, sectors)
+        product = jnp.dot(left_ref[slot], wave[away], preferred_element_type=F32).astype(BF16)
+        return jnp.where(slot < count, product, jnp.zeros_like(product))
+
+    total, ahead = None, halfway(0)
     for slot in range(slots):
-        away = scalars_ref[slot]
-        halfway = jnp.dot(left_ref[slot], wave[jnp.maximum(away, 0)], preferred_element_type=F32).astype(BF16)
-        halfways.append(jnp.where(away >= 0, halfway, jnp.zeros_like(halfway)))
-    total = None
-    for slot in range(slots):
+        current, ahead = ahead, halfway(slot + 1) if slot + 1 < slots else None
         copies[slot].wait()
         product = lax.dot_general(
-            halfways[slot], right_ref[slot], (((1,), (1,)), ((), ())), preferred_element_type=F32
+            current, right_ref[slot], (((1,), (1,)), ((), ())), preferred_element_type=F32
         )
         total = product if total is None else total + product
     for place, block in enumerate(order):
@@ -93,18 +89,11 @@
     groups = [[far_place * near + i for i in range(near)] for far_place in range(op_devices // near)]
     blocks = [i + spread(p, far[::-1]) for i in range(near) for p in range(op_devices // near)]
 
-    scalars = pl.pallas_call(
-        functools.partial(scalars_kernel, sec_devices),
-        out_shape=jax.ShapeDtypeStruct((slots,), jnp.int32),
-        in_specs=[SMEM] * 2,
-        out_specs=SMEM,
-        compiler_params=pltpu.CompilerParams(vmem_limit_bytes=2**20),
-    )(in_sector, counts.T)
     held = wavefunction[0]
     for step, mask in enumerate(far[::-1]):
         arrived = exchange(held, "op", mask)
         if step == 0:
-            held, scalars = lax.optimization_barrier((load(held), scalars))
+            held = load(held)
         there = (op_place & mask) != 0
         held = jnp.concatenate(
             [jnp.where(there, arrived, held), jnp.where(there, held, arrived)], axis=0
@@ -126,7 +115,7 @@
     summed = pl.pallas_call(
         functools.partial(terms_kernel, blocks),
         out_shape=jax.ShapeDtypeStruct((near, left_rows // near, order), BF16),
-        in_specs=[SMEM, VMEM, HBM] + [VMEM] * sec_devices,
+        in_specs=[SMEM, SMEM, VMEM, HBM] + [VMEM] * sec_devices,
         out_specs=VMEM,
         scratch_shapes=[
             pltpu.VMEM((sec_devices, order, order), BF16),
@@ -135,7 +124,7 @@
         ],
         compiler_params=pltpu.CompilerParams(vmem_limit_bytes=49 * 2**20),
         cost_estimate=costs(4 * slots * left_rows * order, 4 * slots * left_rows * order * order),
-    )(scalars, left_ops, right_ops, own, *gathered[1:])
+    )(in_sector, counts.T, left_ops, right_ops, own, *gathered[1:])
 
     parts = lax.all_to_all(summed, "op", 0, 0, axis_index_groups=groups)
     keep = jnp.sum(parts.astype(F32), axis=0)

time: 45.8 us -> 43.6 us (0.952)
  starting transfers between devices: 5.14 us -> 6.9 us
  Pallas kernels: 5.64 us -> 4.02 us
  local copies, waits for them, and re-layouts: 2.16 us -> 0.84 us
  blocking collectives: 26.1 us -> 25.2 us
    ppermute x2, starting transfers between devices: 5.14 us -> 6.9 us  [exchange(): return lax.ppermute(value, axis, [(i, i ^ mask) for i in range(size)])]
    unnamed x8, local copies, waits for them, and re-layouts: 2.12 us -> 0.8 us
    pallas_call x1 -> x0, Pallas kernels: 1.17 us -> none  [shards(): pl.pallas_call(functools.partial(scalars_kernel, sec_devices), out_shape=...]
    all_to_all x1, blocking collectives: 13.7 us -> 12.8 us  [shards(): gathered = [lax.all_to_all(held, 'op', 0, 0, axis_index_groups=groups)]]
    pallas_call x1, Pallas kernels: 4.42 us -> 3.96 us  [shards(): pl.pallas_call(functools.partial(terms_kernel, blocks), out_shape=jax.Sha...]
  transfers between devices with their start and end apart: 3 -> 3, of which waited for: 2 -> 3; matrix products, arithmetic and copies ran while one was open for 0% -> 0% of each run, Pallas kernels for 3% -> 0%
where the time goes in v5:
time: 43.6 us; the launch traced here: 43.3 us
  blocking collectives  25.2 us (58%)
  starting transfers between devices  6.9 us (16%)
  waiting for transfers between devices  5.51 us (13%)
  Pallas kernels  4.02 us (9%)
  local copies, waits for them, and re-layouts  0.84 us (2%)
  other arithmetic  0.73 us (2%)
    all_to_all x1, blocking collectives, shards(): gathered = [lax.all_to_all(held, 'op', 0, 0, axis_index_groups=groups)]  12.8 us
    all_to_all x1, blocking collectives, shards(): parts = lax.all_to_all(summed, 'op', 0, 0, axis_index_groups=groups)  12.4 us
    ppermute x2, starting transfers between devices, exchange(): return lax.ppermute(value, axis, [(i, i ^ mask) for i in range(size)])  6.9 us
    pallas_call x1, Pallas kernels, shards(): pl.pallas_call(functools.partial(terms_kernel, blocks), out_shape=jax.Sha...  3.96 us
    ppermute x2, waiting for transfers between devices, exchange(): return lax.ppermute(value, axis, [(i, i ^ mask) for i in range(size)])  3.64 us
    ppermute x1, waiting for transfers between devices, shards(): gathered.append(lax.ppermute(gathered[0], 'sec', turn))  1.87 us
  transfers between devices with their start and end apart: 3, of which 3 were waited for; matrix products, arithmetic and copies ran while one was open for 0% of the time, Pallas kernels for 0%

profile of v5, /device:TPU:0, one launch (start us, length us, event | category | flops | bytes accessed | tf_op | source)
XLA Modules:
  0.0 43.3 jit_solution(1760894696278549811)
XLA Ops:
  0.0 0.0 copy-start.2
  0.0 0.0 copy-start.3
  0.0 4.0 %collective-permute-start = (bf16[32,512]{1,0:T(8,128)(2,1)}, bf16[32,512]{1,0:T(8,128)(2,1)S(1)}, u32[]{:S(2)}, u32[]{:S(2)}) collective-permute-start(bf16[32,512]{1,0:T(8,128)(2,1)} %bitcast.4), channel_id=1, source_target_pairs={{0,16},{2,18},{4,20},{6,22},{8,24},{10,26},{12,28},{14,30},{16,0},... | collective-permute-start | bytes 98312 | tf_op jit(solution)/shard_map/ppermute | solution.py:18
  4.0 0.0 copy-start
  4.0 0.8 %copy-done = bf16[1,32,512]{2,1,0:T(8,128)(2,1)S(1)} copy-done((bf16[1,32,512]{2,1,0:T(8,128)(2,1)S(1)}, bf16[1,32,512]{2,1,0:T(8,128)(2,1)}, u32[]{:S(2)}) %copy-start) | copy-done | bytes 32792
  4.8 0.0 copy-start.1
  4.9 1.6 %collective-permute-done = bf16[32,512]{1,0:T(8,128)(2,1)S(1)} collective-permute-done((bf16[32,512]{1,0:T(8,128)(2,1)}, bf16[32,512]{1,0:T(8,128)(2,1)S(1)}, u32[]{:S(2)}, u32[]{:S(2)}) %collective-permute-start) | collective-permute-done | bytes 32800 | tf_op jit(solution)/shard_map/ppermute | solution.py:18
  6.6 12.8 %all_to_all.10.source = bf16[8,64,512]{2,1,0:T(8,128)(2,1)S(1)} all-to-all(bf16[8,64,512]{2,1,0:T(8,128)(2,1)S(1)} %broadcast_in_dim.4), channel_id=1, replica_groups={{0,2,4,6,8,10,12,14},{16,18,20,22,24,26,28,30},{1,3,5,7,9,11,13,15},{17..., dimensions={0} | all-to-all | bytes 1048576 | tf_op jit(solution)/shard_map/all_to_all | solution.py:102
  19.4 0.0 collective-permute-start.1
  19.4 1.9 %collective-permute-done.1.refs_0_ = bf16[8,64,512]{2,1,0:T(8,128)(2,1)S(1)} collective-permute-done((bf16[8,64,512]{2,1,0:T(8,128)(2,1)S(1)}, bf16[8,64,512]{2,1,0:T(8,128)(2,1)S(1)}, u32[]{:S(2)}, u32[]{:S(2)}) %collective-permute-start.1) | collective-permute-done | bytes 524320 | tf_op jit(solution)/shard_map/ppermute | solution.py:105
  21.3 0.0 copy-done.2
  21.3 0.0 copy-done.3
  21.3 0.0 copy-done.1
  21.3 4.0 %shard_map.57 = bf16[8,64,512]{2,1,0:T(8,128)(2,1)S(1)} custom-call(s32[4]{0:T(128)S(1)} %copy-done.3, s32[2,16]{1,0:T(2,128)S(1)} %bitcast.6, bf16[4,512,512]{2,1,0:T(8,128)(2,1)S(1)} %copy-done.1, bf16[4,512,512]{2,1,0:T(8,128)(2,1)} %right_hbm.1, bf16[512,512]{1,0:T(8,128)(2,1)S(1)} %shard_map.56.own_ref, ...), custom_call_target="tpu_custom_call" | custom-call | flops 2147483648 | bytes 4194304 | tf_op jit(solution)/shard_map/pallas_call | solution.py:115
  25.3 12.4 %all_to_all.11 = bf16[8,64,512]{2,1,0:T(8,128)(2,1)S(1)} all-to-all(bf16[8,64,512]{2,1,0:T(8,128)(2,1)S(1)} %shard_map.57), channel_id=1, replica_groups={{0,2,4,6,8,10,12,14},{16,18,20,22,24,26,28,30},{1,3,5,7,9,11,13,15},{17..., dimensions={0} | all-to-all | bytes 1048576 | tf_op jit(solution)/shard_map/all_to_all | solution.py:129
  37.7 0.1 convert_reduce_fusion
  37.8 2.9 %collective-permute-start.2 = (bf16[32,512]{1,0:T(8,128)(2,1)S(1)}, bf16[32,512]{1,0:T(8,128)(2,1)S(1)}, u32[]{:S(2)}, u32[]{:S(2)}) collective-permute-start(bf16[32,512]{1,0:T(8,128)(2,1)S(1)} %select_convert_fusion), channel_id=1, source_target_pairs={{0,16},{2,18},{4,20},{6,22},{8,24},{10,26},{12,28},{14,30},{16,0},... | collective-permute-start | bytes 98312 | tf_op jit(solution)/shard_map/ppermute | solution.py:18
  40.6 2.0 %collective-permute-done.2 = bf16[32,512]{1,0:T(8,128)(2,1)S(1)} collective-permute-done((bf16[32,512]{1,0:T(8,128)(2,1)S(1)}, bf16[32,512]{1,0:T(8,128)(2,1)S(1)}, u32[]{:S(2)}, u32[]{:S(2)}) %collective-permute-start.2) | collective-permute-done | bytes 32800 | tf_op jit(solution)/shard_map/ppermute | solution.py:18
  42.7 0.6 %fusion = bf16[1,32,512]{2,1,0:T(8,128)(2,1)} fusion(bf16[32,512]{1,0:T(8,128)(2,1)S(1)} %collective-permute-done.2, f32[64,512]{1,0:T(8,128)S(1)} %convert_reduce_fusion, pred[]{:T(512)S(6)} %ne.4), kind=kLoop, calls=%fused_computation.4 | loop fusion | flops 81920 | bytes 196609 | tf_op jit(solution)/shard_map/broadcast_in_dim | solution.py:137
  (6 shorter events, 0.1 us)
Async XLA Ops:
  0.0 21.3 %copy-start.2 = (s32[16,2]{0,1:T(2,128)S(1)}, s32[16,2]{0,1:T(2,128)}, u32[]{:S(2)}) copy-start(s32[16,2]{0,1:T(2,128)} %param.9) | copy-start | bytes 388
  0.0 21.3 %copy-start.3 = (s32[4]{0:T(128)S(1)}, s32[4]{0:T(128)}, u32[]{:S(2)}) copy-start(s32[4]{0:T(128)} %sector_ref.1) | copy-start | bytes 52
  0.0 6.5 %collective-permute-start = (bf16[32,512]{1,0:T(8,128)(2,1)}, bf16[32,512]{1,0:T(8,128)(2,1)S(1)}, u32[]{:S(2)}, u32[]{:S(2)}) collective-permute-start(bf16[32,512]{1,0:T(8,128)(2,1)} %bitcast.4), channel_id=1, source_target_pairs={{0,16},{2,18},{4,20},{6,22},{8,24},{10,26},{12,28},{14,30},{16,0},... | collective-permute-start | bytes 98312 | tf_op jit(solution)/shard_map/ppermute | solution.py:18
  4.0 0.8 %copy-start = (bf16[1,32,512]{2,1,0:T(8,128)(2,1)S(1)}, bf16[1,32,512]{2,1,0:T(8,128)(2,1)}, u32[]{:S(2)}) copy-start(bf16[1,32,512]{2,1,0:T(8,128)(2,1)} %param.5) | copy-start | bytes 98308
  4.8 16.5 %copy-start.1 = (bf16[4,512,512]{2,1,0:T(8,128)(2,1)S(1)}, bf16[4,512,512]{2,1,0:T(8,128)(2,1)}, u32[]{:S(2)}) copy-start(bf16[4,512,512]{2,1,0:T(8,128)(2,1)} %left_ref.1) | copy-start | bytes 6291460
  19.4 1.9 %collective-permute-start.1 = (bf16[8,64,512]{2,1,0:T(8,128)(2,1)S(1)}, bf16[8,64,512]{2,1,0:T(8,128)(2,1)S(1)}, u32[]{:S(2)}, u32[]{:S(2)}) collective-permute-start(bf16[8,64,512]{2,1,0:T(8,128)(2,1)S(1)} %all_to_all.10.source), channel_id=1, source_target_pairs={{0,1},{1,0},{2,3},{3,2},{4,5},{5,4},{6,7},{7,6},{8,9},{9,8},{10,11... | collective-permute-start | bytes 1572872 | tf_op jit(solution)/shard_map/ppermute | solution.py:105
  37.8 4.9 %collective-permute-start.2 = (bf16[32,512]{1,0:T(8,128)(2,1)S(1)}, bf16[32,512]{1,0:T(8,128)(2,1)S(1)}, u32[]{:S(2)}, u32[]{:S(2)}) collective-permute-start(bf16[32,512]{1,0:T(8,128)(2,1)S(1)} %select_convert_fusion), channel_id=1, source_target_pairs={{0,16},{2,18},{4,20},{6,22},{8,24},{10,26},{12,28},{14,30},{16,0},... | collective-permute-start | bytes 98312 | tf_op jit(solution)/shard_map/ppermute | solution.py:18

commit v6 on v5

--- a/solution.py
+++ b/solution.py
@@ -11,6 +11,8 @@
 SMEM = pl.BlockSpec(memory_space=pltpu.SMEM)
 VMEM = pl.BlockSpec(memory_space=pltpu.VMEM)
 HBM = pl.BlockSpec(memory_space=pltpu.HBM)
+GATHER_NEAR, SCATTER_NEAR = 8, 8
+READY_LIMIT = 49 * 2**20
 
 
 def exchange(value, axis, mask):
@@ -50,32 +52,31 @@
         place[block * rows : (block + 1) * rows, :] = source[group, part : part + rows, :]
 
 
-def terms_kernel(order, sector_ref, counts_ref, left_ref, right_hbm, own_ref, *refs):
-    others, (sum_ref, wave, right_ref, sems) = refs[:-4], refs[-4:]
+def ready_kernel(order, right_hbm, source, right_ref, own_ref, sem):
+    copy = pltpu.make_async_copy(right_hbm, right_ref, sem)
+    copy.start()
+    in_order(order, own_ref.shape[0] // len(order), source, own_ref)
+    copy.wait()
+
+
+def terms_kernel(order, sum_order, sector_ref, counts_ref, left_ref, right_ref, own_ref, *refs):
+    others, (sum_ref, wave) = refs[:-2], refs[-2:]
     slots, rows, sectors = left_ref.shape[0], left_ref.shape[1] // len(order), wave.shape[0]
-    copies = [pltpu.make_async_copy(right_hbm.at[t], right_ref.at[t], sems.at[t]) for t in range(slots)]
-    for copy in copies:
-        copy.start()
     wave[0] = own_ref[...]
     for away, ref in enumerate(others):
         in_order(order, rows, ref, wave.at[away + 1])
     sector = lax.axis_index("sec")
     count = counts_ref[sector, lax.axis_index("op")]
-
-    def halfway(slot):
+    total = None
+    for slot in range(slots):
         away = lax.rem(sector - sector_ref[slot] + sectors, sectors)
-        product = jnp.dot(left_ref[slot], wave[away], preferred_element_type=F32).astype(BF16)
-        return jnp.where(slot < count, product, jnp.zeros_like(product))
-
-    total, ahead = None, halfway(0)
-    for slot in range(slots):
-        current, ahead = ahead, halfway(slot + 1) if slot + 1 < slots else None
-        copies[slot].wait()
+        halfway = jnp.dot(left_ref[slot], wave[away], preferred_element_type=F32).astype(BF16)
+        halfway = jnp.where(slot < count, halfway, jnp.zeros_like(halfway))
         product = lax.dot_general(
-            current, right_ref[slot], (((1,), (1,)), ((), ())), preferred_element_type=F32
+            halfway, right_ref[slot], (((1,), (1,)), ((), ())), preferred_element_type=F32
         )
         total = product if total is None else total + product
-    for place, block in enumerate(order):
+    for place, block in enumerate(sum_order):
         group, part = divmod(place * rows, sum_ref.shape[1])
         sum_ref[group, part : part + rows, :] = total[block * rows : (block + 1) * rows, :].astype(BF16)
 
@@ -84,11 +85,16 @@
     op_devices, sec_devices = lax.axis_size("op"), lax.axis_size("sec")
     op_place = lax.axis_index("op")
     slots, left_rows, order = left_ops.shape
-    near = min(8, op_devices) if op_devices & (op_devices - 1) == 0 else op_devices
-    far = [near << bit for bit in range((op_devices // near).bit_length() - 1)]
-    groups = [[far_place * near + i for i in range(near)] for far_place in range(op_devices // near)]
-    blocks = [i + spread(p, far[::-1]) for i in range(near) for p in range(op_devices // near)]
+    def split(near):
+        if op_devices & (op_devices - 1):
+            near = op_devices
+        near = min(near, op_devices)
+        far = [near << bit for bit in range((op_devices // near).bit_length() - 1)]
+        groups = [[place * near + i for i in range(near)] for place in range(op_devices // near)]
+        blocks = [i + spread(p, far[::-1]) for i in range(near) for p in range(op_devices // near)]
+        return near, far, groups, blocks
 
+    near, far, groups, blocks = split(GATHER_NEAR)
     held = wavefunction[0]
     for step, mask in enumerate(far[::-1]):
         arrived = exchange(held, "op", mask)
@@ -103,28 +109,29 @@
     for away in range(1, sec_devices):
         turn = [(i, (i + away) % sec_devices) for i in range(sec_devices)]
         gathered.append(lax.ppermute(gathered[0], "sec", turn))
-    own = pl.pallas_call(
-        functools.partial(in_order, blocks, left_rows // op_devices),
-        out_shape=jax.ShapeDtypeStruct((order, order), BF16),
-        in_specs=[VMEM],
+    right, own = pl.pallas_call(
+        functools.partial(ready_kernel, blocks),
+        out_shape=(
+            jax.ShapeDtypeStruct(right_ops.shape, BF16),
+            jax.ShapeDtypeStruct((order, order), BF16),
+        ),
+        in_specs=[HBM, VMEM],
+        out_specs=(VMEM, VMEM),
+        scratch_shapes=[pltpu.SemaphoreType.DMA],
+        compiler_params=pltpu.CompilerParams(vmem_limit_bytes=READY_LIMIT),
+        cost_estimate=costs(4 * slots * left_rows * order),
+    )(right_ops, gathered[0])
+
+    near, far, groups, sum_blocks = split(SCATTER_NEAR)
+    summed = pl.pallas_call(
+        functools.partial(terms_kernel, blocks, sum_blocks),
+        out_shape=jax.ShapeDtypeStruct((near, left_rows // near, order), BF16),
+        in_specs=[SMEM] * 2 + [VMEM] * (2 + sec_devices),
         out_specs=VMEM,
-        compiler_params=pltpu.CompilerParams(vmem_limit_bytes=2**20),
-        cost_estimate=costs(4 * slots * left_rows * order),
-    )(gathered[0])
-
-    summed = pl.pallas_call(
-        functools.partial(terms_kernel, blocks),
-        out_shape=jax.ShapeDtypeStruct((near, left_rows // near, order), BF16),
-        in_specs=[SMEM, SMEM, VMEM, HBM] + [VMEM] * sec_devices,
-        out_specs=VMEM,
-        scratch_shapes=[
-            pltpu.VMEM((sec_devices, order, order), BF16),
-            pltpu.VMEM(right_ops.shape, BF16),
-            pltpu.SemaphoreType.DMA((slots,)),
-        ],
-        compiler_params=pltpu.CompilerParams(vmem_limit_bytes=49 * 2**20),
+        scratch_shapes=[pltpu.VMEM((sec_devices, order, order), BF16)],
+        compiler_params=pltpu.CompilerParams(vmem_limit_bytes=16 * 2**20),
         cost_estimate=costs(4 * slots * left_rows * order, 4 * slots * left_rows * order * order),
-    )(in_sector, counts.T, left_ops, right_ops, own, *gathered[1:])
+    )(in_sector, counts.T, left_ops, right, own, *gathered[1:])
 
     parts = lax.all_to_all(summed, "op", 0, 0, axis_index_groups=groups)
     keep = jnp.sum(parts.astype(F32), axis=0)

time: 43.6 us -> 42.8 us (0.982)
  waiting for transfers between devices: 5.51 us -> 3.95 us
  Pallas kernels: 4.02 us -> 4.56 us
    ppermute x1, waiting for transfers between devices: 1.87 us -> 0.3 us  [shards(): gathered.append(lax.ppermute(gathered[0], 'sec', turn))]
    pallas_call x2, Pallas kernels: 4 us -> 4.54 us  [the longest x1 2.94 us: shards(): pl.pallas_call(functools.partial(terms_kernel, blocks, sum_blocks), out_s...]
  transfers between devices with their start and end apart: 3 -> 3, of which waited for: 3 -> 3; matrix products, arithmetic and copies ran while one was open for 0% -> 0% of each run, Pallas kernels for 0% -> 4%
where the time goes in v6:
time: 42.8 us; the launch traced here: 42.5 us
  blocking collectives  25.5 us (60%)
  starting transfers between devices  6.9 us (16%)
  Pallas kernels  4.56 us (11%)
  waiting for transfers between devices  3.95 us (9%)
  local copies, waits for them, and re-layouts  0.85 us (2%)
  other arithmetic  0.73 us (2%)
    all_to_all x1, blocking collectives, shards(): gathered = [lax.all_to_all(held, 'op', 0, 0, axis_index_groups=groups)]  12.9 us
    all_to_all x1, blocking collectives, shards(): parts = lax.all_to_all(summed, 'op', 0, 0, axis_index_groups=groups)  12.5 us
    ppermute x2, starting transfers between devices, exchange(): return lax.ppermute(value, axis, [(i, i ^ mask) for i in range(size)])  6.9 us
    ppermute x2, waiting for transfers between devices, exchange(): return lax.ppermute(value, axis, [(i, i ^ mask) for i in range(size)])  3.65 us
    pallas_call x1, Pallas kernels, shards(): pl.pallas_call(functools.partial(terms_kernel, blocks, sum_blocks), out_s...  2.94 us
    pallas_call x1, Pallas kernels, shards(): pl.pallas_call(functools.partial(ready_kernel, blocks), out_shape=(jax.Sh...  1.6 us
  transfers between devices with their start and end apart: 3, of which 3 were waited for; matrix products, arithmetic and copies ran while one was open for 0% of the time, Pallas kernels for 4%

profile of v6, /device:TPU:0, one launch (start us, length us, event | category | flops | bytes accessed | tf_op | source)
XLA Modules:
  0.0 42.5 jit_solution(17057417761065322554)
XLA Ops:
  0.0 4.0 %collective-permute-start = (bf16[32,512]{1,0:T(8,128)(2,1)}, bf16[32,512]{1,0:T(8,128)(2,1)S(1)}, u32[]{:S(2)}, u32[]{:S(2)}) collective-permute-start(bf16[32,512]{1,0:T(8,128)(2,1)} %bitcast.4), channel_id=1, source_target_pairs={{0,16},{2,18},{4,20},{6,22},{8,24},{10,26},{12,28},{14,30},{16,0},... | collective-permute-start | bytes 98312 | tf_op jit(solution)/shard_map/ppermute | solution.py:20
  4.0 0.0 copy-start
  4.0 0.8 %copy-done = bf16[1,32,512]{2,1,0:T(8,128)(2,1)S(1)} copy-done((bf16[1,32,512]{2,1,0:T(8,128)(2,1)S(1)}, bf16[1,32,512]{2,1,0:T(8,128)(2,1)}, u32[]{:S(2)}) %copy-start) | copy-done | bytes 32792
  4.9 1.6 %collective-permute-done = bf16[32,512]{1,0:T(8,128)(2,1)S(1)} collective-permute-done((bf16[32,512]{1,0:T(8,128)(2,1)}, bf16[32,512]{1,0:T(8,128)(2,1)S(1)}, u32[]{:S(2)}, u32[]{:S(2)}) %collective-permute-start) | collective-permute-done | bytes 32800 | tf_op jit(solution)/shard_map/ppermute | solution.py:20
  6.5 0.0 copy-start.1
  6.5 0.0 copy-start.2
  6.5 0.0 copy-start.3
  6.6 12.9 %all_to_all.10.source = bf16[8,64,512]{2,1,0:T(8,128)(2,1)S(1)} all-to-all(bf16[8,64,512]{2,1,0:T(8,128)(2,1)S(1)} %broadcast_in_dim.4), channel_id=1, replica_groups={{0,2,4,6,8,10,12,14},{16,18,20,22,24,26,28,30},{1,3,5,7,9,11,13,15},{17..., dimensions={0} | all-to-all | bytes 1048576 | tf_op jit(solution)/shard_map/all_to_all | solution.py:108
  19.5 0.0 collective-permute-start.1
  19.5 1.6 %shard_map.56 = (bf16[4,512,512]{2,1,0:T(8,128)(2,1)S(1)}, bf16[512,512]{1,0:T(8,128)(2,1)S(1)}) custom-call(bf16[4,512,512]{2,1,0:T(8,128)(2,1)} %right_hbm.1, bf16[8,64,512]{2,1,0:T(8,128)(2,1)S(1)} %all_to_all.10.source), custom_call_target="tpu_custom_call" | custom-call | bytes 4194304 | tf_op jit(solution)/shard_map/pallas_call | solution.py:112
  21.1 0.3 collective-permute-done.1.refs_0_
  21.4 0.0 copy-done.1
  21.5 0.0 copy-done.2
  21.5 0.0 copy-done.3
  21.5 2.9 %shard_map.57 = bf16[8,64,512]{2,1,0:T(8,128)(2,1)S(1)} custom-call(s32[4]{0:T(128)S(1)} %copy-done.3, s32[2,16]{1,0:T(2,128)S(1)} %bitcast.6, bf16[4,512,512]{2,1,0:T(8,128)(2,1)S(1)} %copy-done.1, bf16[4,512,512]{2,1,0:T(8,128)(2,1)S(1)} %get-tuple-element.7.right_ref, bf16[512,512]{1,0:T(8,128)(2,1)S(1)} %get-tuple-element.8.own_ref, ...), custom_call_target="tpu_custom_call" | custom-call | flops 2147483648 | bytes 4194304 | tf_op jit(solution)/shard_map/pallas_call | solution.py:126
  24.4 12.5 %all_to_all.11 = bf16[8,64,512]{2,1,0:T(8,128)(2,1)S(1)} all-to-all(bf16[8,64,512]{2,1,0:T(8,128)(2,1)S(1)} %shard_map.57), channel_id=1, replica_groups={{0,2,4,6,8,10,12,14},{16,18,20,22,24,26,28,30},{1,3,5,7,9,11,13,15},{17..., dimensions={0} | all-to-all | bytes 1048576 | tf_op jit(solution)/shard_map/all_to_all | solution.py:136
  36.9 0.1 convert_reduce_fusion
  37.0 2.9 %collective-permute-start.2 = (bf16[32,512]{1,0:T(8,128)(2,1)S(1)}, bf16[32,512]{1,0:T(8,128)(2,1)S(1)}, u32[]{:S(2)}, u32[]{:S(2)}) collective-permute-start(bf16[32,512]{1,0:T(8,128)(2,1)S(1)} %select_convert_fusion), channel_id=1, source_target_pairs={{0,16},{2,18},{4,20},{6,22},{8,24},{10,26},{12,28},{14,30},{16,0},... | collective-permute-start | bytes 98312 | tf_op jit(solution)/shard_map/ppermute | solution.py:20
  39.9 2.0 %collective-permute-done.2 = bf16[32,512]{1,0:T(8,128)(2,1)S(1)} collective-permute-done((bf16[32,512]{1,0:T(8,128)(2,1)S(1)}, bf16[32,512]{1,0:T(8,128)(2,1)S(1)}, u32[]{:S(2)}, u32[]{:S(2)}) %collective-permute-start.2) | collective-permute-done | bytes 32800 | tf_op jit(solution)/shard_map/ppermute | solution.py:20
  41.9 0.6 %fusion = bf16[1,32,512]{2,1,0:T(8,128)(2,1)} fusion(bf16[32,512]{1,0:T(8,128)(2,1)S(1)} %collective-permute-done.2, f32[64,512]{1,0:T(8,128)S(1)} %convert_reduce_fusion, pred[]{:T(512)S(6)} %ne.4), kind=kLoop, calls=%fused_computation.4 | loop fusion | flops 81920 | bytes 196609 | tf_op jit(solution)/shard_map/broadcast_in_dim | solution.py:144
  (5 shorter events, 0.1 us)
Async XLA Ops:
  0.0 6.5 %collective-permute-start = (bf16[32,512]{1,0:T(8,128)(2,1)}, bf16[32,512]{1,0:T(8,128)(2,1)S(1)}, u32[]{:S(2)}, u32[]{:S(2)}) collective-permute-start(bf16[32,512]{1,0:T(8,128)(2,1)} %bitcast.4), channel_id=1, source_target_pairs={{0,16},{2,18},{4,20},{6,22},{8,24},{10,26},{12,28},{14,30},{16,0},... | collective-permute-start | bytes 98312 | tf_op jit(solution)/shard_map/ppermute | solution.py:20
  4.0 0.8 %copy-start = (bf16[1,32,512]{2,1,0:T(8,128)(2,1)S(1)}, bf16[1,32,512]{2,1,0:T(8,128)(2,1)}, u32[]{:S(2)}) copy-start(bf16[1,32,512]{2,1,0:T(8,128)(2,1)} %param.5) | copy-start | bytes 98308
  6.5 14.9 %copy-start.1 = (bf16[4,512,512]{2,1,0:T(8,128)(2,1)S(1)}, bf16[4,512,512]{2,1,0:T(8,128)(2,1)}, u32[]{:S(2)}) copy-start(bf16[4,512,512]{2,1,0:T(8,128)(2,1)} %left_ref.1) | copy-start | bytes 6291460
  6.5 14.9 %copy-start.2 = (s32[16,2]{0,1:T(2,128)S(1)}, s32[16,2]{0,1:T(2,128)}, u32[]{:S(2)}) copy-start(s32[16,2]{0,1:T(2,128)} %param.9) | copy-start | bytes 388
  6.5 14.9 %copy-start.3 = (s32[4]{0:T(128)S(1)}, s32[4]{0:T(128)}, u32[]{:S(2)}) copy-start(s32[4]{0:T(128)} %sector_ref.1) | copy-start | bytes 52
  19.5 1.9 %collective-permute-start.1 = (bf16[8,64,512]{2,1,0:T(8,128)(2,1)S(1)}, bf16[8,64,512]{2,1,0:T(8,128)(2,1)S(1)}, u32[]{:S(2)}, u32[]{:S(2)}) collective-permute-start(bf16[8,64,512]{2,1,0:T(8,128)(2,1)S(1)} %all_to_all.10.source), channel_id=1, source_target_pairs={{0,1},{1,0},{2,3},{3,2},{4,5},{5,4},{6,7},{7,6},{8,9},{9,8},{10,11... | collective-permute-start | bytes 1572872 | tf_op jit(solution)/shard_map/ppermute | solution.py:111
  37.0 4.9 %collective-permute-start.2 = (bf16[32,512]{1,0:T(8,128)(2,1)S(1)}, bf16[32,512]{1,0:T(8,128)(2,1)S(1)}, u32[]{:S(2)}, u32[]{:S(2)}) collective-permute-start(bf16[32,512]{1,0:T(8,128)(2,1)S(1)} %select_convert_fusion), channel_id=1, source_target_pairs={{0,16},{2,18},{4,20},{6,22},{8,24},{10,26},{12,28},{14,30},{16,0},... | collective-permute-start | bytes 98312 | tf_op jit(solution)/shard_map/ppermute | solution.py:20

commit v7 on v6

--- a/solution.py
+++ b/solution.py
@@ -11,7 +11,7 @@
 SMEM = pl.BlockSpec(memory_space=pltpu.SMEM)
 VMEM = pl.BlockSpec(memory_space=pltpu.VMEM)
 HBM = pl.BlockSpec(memory_space=pltpu.HBM)
-GATHER_NEAR, SCATTER_NEAR = 8, 8
+NEAR_ORDER = (0, 7, 5, 3, 1, 6, 4, 2)
 READY_LIMIT = 49 * 2**20
 
 
@@ -59,7 +59,7 @@
     copy.wait()
 
 
-def terms_kernel(order, sum_order, sector_ref, counts_ref, left_ref, right_ref, own_ref, *refs):
+def terms_kernel(order, sector_ref, counts_ref, left_ref, right_ref, own_ref, *refs):
     others, (sum_ref, wave) = refs[:-2], refs[-2:]
     slots, rows, sectors = left_ref.shape[0], left_ref.shape[1] // len(order), wave.shape[0]
     wave[0] = own_ref[...]
@@ -76,7 +76,7 @@
             halfway, right_ref[slot], (((1,), (1,)), ((), ())), preferred_element_type=F32
         )
         total = product if total is None else total + product
-    for place, block in enumerate(sum_order):
+    for place, block in enumerate(order):
         group, part = divmod(place * rows, sum_ref.shape[1])
         sum_ref[group, part : part + rows, :] = total[block * rows : (block + 1) * rows, :].astype(BF16)
 
@@ -85,16 +85,12 @@
     op_devices, sec_devices = lax.axis_size("op"), lax.axis_size("sec")
     op_place = lax.axis_index("op")
     slots, left_rows, order = left_ops.shape
-    def split(near):
-        if op_devices & (op_devices - 1):
-            near = op_devices
-        near = min(near, op_devices)
-        far = [near << bit for bit in range((op_devices // near).bit_length() - 1)]
-        groups = [[place * near + i for i in range(near)] for place in range(op_devices // near)]
-        blocks = [i + spread(p, far[::-1]) for i in range(near) for p in range(op_devices // near)]
-        return near, far, groups, blocks
+    ring = NEAR_ORDER if op_devices % 8 == 0 and op_devices & (op_devices - 1) == 0 else range(op_devices)
+    near = len(ring)
+    far = [near << bit for bit in range((op_devices // near).bit_length() - 1)]
+    groups = [[place * near + i for i in ring] for place in range(op_devices // near)]
+    blocks = [i + spread(p, far[::-1]) for i in ring for p in range(op_devices // near)]
 
-    near, far, groups, blocks = split(GATHER_NEAR)
     held = wavefunction[0]
     for step, mask in enumerate(far[::-1]):
         arrived = exchange(held, "op", mask)
@@ -122,9 +118,8 @@
         cost_estimate=costs(4 * slots * left_rows * order),
     )(right_ops, gathered[0])
 
-    near, far, groups, sum_blocks = split(SCATTER_NEAR)
     summed = pl.pallas_call(
-        functools.partial(terms_kernel, blocks, sum_blocks),
+        functools.partial(terms_kernel, blocks),
         out_shape=jax.ShapeDtypeStruct((near, left_rows // near, order), BF16),
         in_specs=[SMEM] * 2 + [VMEM] * (2 + sec_devices),
         out_specs=VMEM,

time: 42.8 us -> 41.4 us (0.967)
  blocking collectives: 25.5 us -> 24 us
    all_to_all x1, blocking collectives: 12.5 us -> 11.8 us  [shards(): parts = lax.all_to_all(summed, 'op', 0, 0, axis_index_groups=groups)]
    all_to_all x1, blocking collectives: 12.9 us -> 12.2 us  [shards(): gathered = [lax.all_to_all(held, 'op', 0, 0, axis_index_groups=groups)]]
where the time goes in v7:
time: 41.4 us; the launch traced here: 41.1 us
  blocking collectives  24 us (58%)
  starting transfers between devices  6.91 us (17%)
  Pallas kernels  4.56 us (11%)
  waiting for transfers between devices  3.93 us (9%)
  local copies, waits for them, and re-layouts  0.85 us (2%)
  other arithmetic  0.73 us (2%)
    all_to_all x1, blocking collectives, shards(): gathered = [lax.all_to_all(held, 'op', 0, 0, axis_index_groups=groups)]  12.2 us
    all_to_all x1, blocking collectives, shards(): parts = lax.all_to_all(summed, 'op', 0, 0, axis_index_groups=groups)  11.8 us
    ppermute x2, starting transfers between devices, exchange(): return lax.ppermute(value, axis, [(i, i ^ mask) for i in range(size)])  6.91 us
    ppermute x2, waiting for transfers between devices, exchange(): return lax.ppermute(value, axis, [(i, i ^ mask) for i in range(size)])  3.63 us
    pallas_call x1, Pallas kernels, shards(): pl.pallas_call(functools.partial(terms_kernel, blocks), out_shape=jax.Sha...  2.94 us
    pallas_call x1, Pallas kernels, shards(): pl.pallas_call(functools.partial(ready_kernel, blocks), out_shape=(jax.Sh...  1.6 us
  transfers between devices with their start and end apart: 3, of which 3 were waited for; matrix products, arithmetic and copies ran while one was open for 0% of the time, Pallas kernels for 4%

profile of v7, /device:TPU:0, one launch (start us, length us, event | category | flops | bytes accessed | tf_op | source)
XLA Modules:
  0.0 41.1 jit_solution(13089954077732241486)
XLA Ops:
  0.0 4.0 %collective-permute-start = (bf16[32,512]{1,0:T(8,128)(2,1)}, bf16[32,512]{1,0:T(8,128)(2,1)S(1)}, u32[]{:S(2)}, u32[]{:S(2)}) collective-permute-start(bf16[32,512]{1,0:T(8,128)(2,1)} %bitcast.4), channel_id=1, source_target_pairs={{0,16},{2,18},{4,20},{6,22},{8,24},{10,26},{12,28},{14,30},{16,0},... | collective-permute-start | bytes 98312 | tf_op jit(solution)/shard_map/ppermute | solution.py:20
  4.0 0.0 copy-start
  4.0 0.8 %copy-done = bf16[1,32,512]{2,1,0:T(8,128)(2,1)S(1)} copy-done((bf16[1,32,512]{2,1,0:T(8,128)(2,1)S(1)}, bf16[1,32,512]{2,1,0:T(8,128)(2,1)}, u32[]{:S(2)}) %copy-start) | copy-done | bytes 32792
  4.9 1.6 %collective-permute-done = bf16[32,512]{1,0:T(8,128)(2,1)S(1)} collective-permute-done((bf16[32,512]{1,0:T(8,128)(2,1)}, bf16[32,512]{1,0:T(8,128)(2,1)S(1)}, u32[]{:S(2)}, u32[]{:S(2)}) %collective-permute-start) | collective-permute-done | bytes 32800 | tf_op jit(solution)/shard_map/ppermute | solution.py:20
  6.5 0.0 copy-start.1
  6.5 0.0 copy-start.2
  6.5 0.0 copy-start.3
  6.6 12.2 %all_to_all.10.source = bf16[8,64,512]{2,1,0:T(8,128)(2,1)S(1)} all-to-all(bf16[8,64,512]{2,1,0:T(8,128)(2,1)S(1)} %broadcast_in_dim.4), channel_id=1, replica_groups={{0,14,10,6,2,12,8,4},{16,30,26,22,18,28,24,20},{1,15,11,7,3,13,9,5},{17..., dimensions={0} | all-to-all | bytes 1048576 | tf_op jit(solution)/shard_map/all_to_all | solution.py:104
  18.8 0.0 collective-permute-start.1
  18.8 1.6 %shard_map.56 = (bf16[4,512,512]{2,1,0:T(8,128)(2,1)S(1)}, bf16[512,512]{1,0:T(8,128)(2,1)S(1)}) custom-call(bf16[4,512,512]{2,1,0:T(8,128)(2,1)} %right_hbm.1, bf16[8,64,512]{2,1,0:T(8,128)(2,1)S(1)} %all_to_all.10.source), custom_call_target="tpu_custom_call" | custom-call | bytes 4194304 | tf_op jit(solution)/shard_map/pallas_call | solution.py:108
  20.4 0.3 collective-permute-done.1.refs_0_
  20.7 0.0 copy-done.1
  20.7 0.0 copy-done.2
  20.7 0.0 copy-done.3
  20.8 2.9 %shard_map.57 = bf16[8,64,512]{2,1,0:T(8,128)(2,1)S(1)} custom-call(s32[4]{0:T(128)S(1)} %copy-done.3, s32[2,16]{1,0:T(2,128)S(1)} %bitcast.6, bf16[4,512,512]{2,1,0:T(8,128)(2,1)S(1)} %copy-done.1, bf16[4,512,512]{2,1,0:T(8,128)(2,1)S(1)} %get-tuple-element.7.right_ref, bf16[512,512]{1,0:T(8,128)(2,1)S(1)} %get-tuple-element.8.own_ref, ...), custom_call_target="tpu_custom_call" | custom-call | flops 2147483648 | bytes 4194304 | tf_op jit(solution)/shard_map/pallas_call | solution.py:121
  23.7 11.8 %all_to_all.11 = bf16[8,64,512]{2,1,0:T(8,128)(2,1)S(1)} all-to-all(bf16[8,64,512]{2,1,0:T(8,128)(2,1)S(1)} %shard_map.57), channel_id=1, replica_groups={{0,14,10,6,2,12,8,4},{16,30,26,22,18,28,24,20},{1,15,11,7,3,13,9,5},{17..., dimensions={0} | all-to-all | bytes 1048576 | tf_op jit(solution)/shard_map/all_to_all | solution.py:131
  35.5 0.1 convert_reduce_fusion
  35.6 2.9 %collective-permute-start.2 = (bf16[32,512]{1,0:T(8,128)(2,1)S(1)}, bf16[32,512]{1,0:T(8,128)(2,1)S(1)}, u32[]{:S(2)}, u32[]{:S(2)}) collective-permute-start(bf16[32,512]{1,0:T(8,128)(2,1)S(1)} %select_convert_fusion), channel_id=1, source_target_pairs={{0,16},{2,18},{4,20},{6,22},{8,24},{10,26},{12,28},{14,30},{16,0},... | collective-permute-start | bytes 98312 | tf_op jit(solution)/shard_map/ppermute | solution.py:20
  38.4 2.0 %collective-permute-done.2 = bf16[32,512]{1,0:T(8,128)(2,1)S(1)} collective-permute-done((bf16[32,512]{1,0:T(8,128)(2,1)S(1)}, bf16[32,512]{1,0:T(8,128)(2,1)S(1)}, u32[]{:S(2)}, u32[]{:S(2)}) %collective-permute-start.2) | collective-permute-done | bytes 32800 | tf_op jit(solution)/shard_map/ppermute | solution.py:20
  40.4 0.6 %fusion = bf16[1,32,512]{2,1,0:T(8,128)(2,1)} fusion(bf16[32,512]{1,0:T(8,128)(2,1)S(1)} %collective-permute-done.2, f32[64,512]{1,0:T(8,128)S(1)} %convert_reduce_fusion, pred[]{:T(512)S(6)} %ne.4), kind=kLoop, calls=%fused_computation.4 | loop fusion | flops 81920 | bytes 196609 | tf_op jit(solution)/shard_map/broadcast_in_dim | solution.py:139
  (5 shorter events, 0.1 us)
Async XLA Ops:
  0.0 6.5 %collective-permute-start = (bf16[32,512]{1,0:T(8,128)(2,1)}, bf16[32,512]{1,0:T(8,128)(2,1)S(1)}, u32[]{:S(2)}, u32[]{:S(2)}) collective-permute-start(bf16[32,512]{1,0:T(8,128)(2,1)} %bitcast.4), channel_id=1, source_target_pairs={{0,16},{2,18},{4,20},{6,22},{8,24},{10,26},{12,28},{14,30},{16,0},... | collective-permute-start | bytes 98312 | tf_op jit(solution)/shard_map/ppermute | solution.py:20
  4.0 0.8 %copy-start = (bf16[1,32,512]{2,1,0:T(8,128)(2,1)S(1)}, bf16[1,32,512]{2,1,0:T(8,128)(2,1)}, u32[]{:S(2)}) copy-start(bf16[1,32,512]{2,1,0:T(8,128)(2,1)} %param.5) | copy-start | bytes 98308
  6.5 14.2 %copy-start.1 = (bf16[4,512,512]{2,1,0:T(8,128)(2,1)S(1)}, bf16[4,512,512]{2,1,0:T(8,128)(2,1)}, u32[]{:S(2)}) copy-start(bf16[4,512,512]{2,1,0:T(8,128)(2,1)} %left_ref.1) | copy-start | bytes 6291460
  6.5 14.2 %copy-start.2 = (s32[16,2]{0,1:T(2,128)S(1)}, s32[16,2]{0,1:T(2,128)}, u32[]{:S(2)}) copy-start(s32[16,2]{0,1:T(2,128)} %param.9) | copy-start | bytes 388
  6.5 14.2 %copy-start.3 = (s32[4]{0:T(128)S(1)}, s32[4]{0:T(128)}, u32[]{:S(2)}) copy-start(s32[4]{0:T(128)} %sector_ref.1) | copy-start | bytes 52
  18.8 1.9 %collective-permute-start.1 = (bf16[8,64,512]{2,1,0:T(8,128)(2,1)S(1)}, bf16[8,64,512]{2,1,0:T(8,128)(2,1)S(1)}, u32[]{:S(2)}, u32[]{:S(2)}) collective-permute-start(bf16[8,64,512]{2,1,0:T(8,128)(2,1)S(1)} %all_to_all.10.source), channel_id=1, source_target_pairs={{0,1},{1,0},{2,3},{3,2},{4,5},{5,4},{6,7},{7,6},{8,9},{9,8},{10,11... | collective-permute-start | bytes 1572872 | tf_op jit(solution)/shard_map/ppermute | solution.py:107
  35.6 4.9 %collective-permute-start.2 = (bf16[32,512]{1,0:T(8,128)(2,1)S(1)}, bf16[32,512]{1,0:T(8,128)(2,1)S(1)}, u32[]{:S(2)}, u32[]{:S(2)}) collective-permute-start(bf16[32,512]{1,0:T(8,128)(2,1)S(1)} %select_convert_fusion), channel_id=1, source_target_pairs={{0,16},{2,18},{4,20},{6,22},{8,24},{10,26},{12,28},{14,30},{16,0},... | collective-permute-start | bytes 98312 | tf_op jit(solution)/shard_map/ppermute | solution.py:20

commit v8 on v7

--- a/solution.py
+++ b/solution.py
@@ -12,7 +12,7 @@
 VMEM = pl.BlockSpec(memory_space=pltpu.VMEM)
 HBM = pl.BlockSpec(memory_space=pltpu.HBM)
 NEAR_ORDER = (0, 7, 5, 3, 1, 6, 4, 2)
-READY_LIMIT = 49 * 2**20
+READY_LIMIT = 46 * 2**20
 
 
 def exchange(value, axis, mask):
@@ -52,28 +52,43 @@
         place[block * rows : (block + 1) * rows, :] = source[group, part : part + rows, :]
 
 
-def ready_kernel(order, right_hbm, source, right_ref, own_ref, sem):
+def distance(slot, sector_ref, counts_ref, sectors):
+    sector = lax.axis_index("sec")
+    away = lax.rem(sector - sector_ref[slot] + sectors, sectors)
+    return jnp.where(slot < counts_ref[sector, lax.axis_index("op")], away, -1)
+
+
+def ready_kernel(sectors, sector_ref, counts_ref, left_ref, right_hbm, own, right_ref, halfway_ref, sem):
     copy = pltpu.make_async_copy(right_hbm, right_ref, sem)
     copy.start()
-    in_order(order, own_ref.shape[0] // len(order), source, own_ref)
+    for slot in range(left_ref.shape[0]):
+        halfway = jnp.dot(left_ref[slot], own[...], preferred_element_type=F32).astype(BF16)
+        is_own = distance(slot, sector_ref, counts_ref, sectors) == 0
+        halfway_ref[slot] = jnp.where(is_own, halfway, jnp.zeros_like(halfway))
     copy.wait()
 
 
 def terms_kernel(order, sector_ref, counts_ref, left_ref, right_ref, own_ref, *refs):
-    others, (sum_ref, wave) = refs[:-2], refs[-2:]
-    slots, rows, sectors = left_ref.shape[0], left_ref.shape[1] // len(order), wave.shape[0]
-    wave[0] = own_ref[...]
+    others, (sum_ref, wave, halfways) = refs[:-3], refs[-3:]
+    slots, rows = left_ref.shape[0], left_ref.shape[1] // len(order)
     for away, ref in enumerate(others):
-        in_order(order, rows, ref, wave.at[away + 1])
-    sector = lax.axis_index("sec")
-    count = counts_ref[sector, lax.axis_index("op")]
+        in_order(order, rows, ref, wave.at[away])
+    for slot in range(slots):
+        away = distance(slot, sector_ref, counts_ref, len(others) + 1)
+
+        @pl.when(away > 0)
+        def _():
+            other = wave[jnp.maximum(away - 1, 0)]
+            halfways[slot] = jnp.dot(left_ref[slot], other, preferred_element_type=F32).astype(BF16)
+
+        @pl.when(away <= 0)
+        def _():
+            halfways[slot] = own_ref[slot]
+
     total = None
     for slot in range(slots):
-        away = lax.rem(sector - sector_ref[slot] + sectors, sectors)
-        halfway = jnp.dot(left_ref[slot], wave[away], preferred_element_type=F32).astype(BF16)
-        halfway = jnp.where(slot < count, halfway, jnp.zeros_like(halfway))
         product = lax.dot_general(
-            halfway, right_ref[slot], (((1,), (1,)), ((), ())), preferred_element_type=F32
+            halfways[slot], right_ref[slot], (((1,), (1,)), ((), ())), preferred_element_type=F32
         )
         total = product if total is None else total + product
     for place, block in enumerate(order):
@@ -105,25 +120,34 @@
     for away in range(1, sec_devices):
         turn = [(i, (i + away) % sec_devices) for i in range(sec_devices)]
         gathered.append(lax.ppermute(gathered[0], "sec", turn))
+    ordered = pl.pallas_call(
+        functools.partial(in_order, blocks, left_rows // op_devices),
+        out_shape=jax.ShapeDtypeStruct((order, order), BF16),
+        in_specs=[VMEM],
+        out_specs=VMEM,
+        compiler_params=pltpu.CompilerParams(vmem_limit_bytes=2**20),
+        cost_estimate=costs(4 * order * order),
+    )(gathered[0])
+    halfway = jax.ShapeDtypeStruct((slots, left_rows, order), BF16)
     right, own = pl.pallas_call(
-        functools.partial(ready_kernel, blocks),
-        out_shape=(
-            jax.ShapeDtypeStruct(right_ops.shape, BF16),
-            jax.ShapeDtypeStruct((order, order), BF16),
-        ),
-        in_specs=[HBM, VMEM],
+        functools.partial(ready_kernel, sec_devices),
+        out_shape=(jax.ShapeDtypeStruct(right_ops.shape, BF16), halfway),
+        in_specs=[SMEM, SMEM, VMEM, HBM, VMEM],
         out_specs=(VMEM, VMEM),
         scratch_shapes=[pltpu.SemaphoreType.DMA],
         compiler_params=pltpu.CompilerParams(vmem_limit_bytes=READY_LIMIT),
         cost_estimate=costs(4 * slots * left_rows * order),
-    )(right_ops, gathered[0])
+    )(in_sector, counts.T, left_ops, right_ops, ordered)
 
     summed = pl.pallas_call(
         functools.partial(terms_kernel, blocks),
         out_shape=jax.ShapeDtypeStruct((near, left_rows // near, order), BF16),
         in_specs=[SMEM] * 2 + [VMEM] * (2 + sec_devices),
         out_specs=VMEM,
-        scratch_shapes=[pltpu.VMEM((sec_devices, order, order), BF16)],
+        scratch_shapes=[
+            pltpu.VMEM((max(sec_devices - 1, 1), order, order), BF16),
+            pltpu.VMEM(halfway.shape, BF16),
+        ],
         compiler_params=pltpu.CompilerParams(vmem_limit_bytes=16 * 2**20),
         cost_estimate=costs(4 * slots * left_rows * order, 4 * slots * left_rows * order * order),
     )(in_sector, counts.T, left_ops, right, own, *gathered[1:])

time: 41.4 us -> 41.8 us (level)
  blocking collectives: 24 us -> 24.8 us
  starting transfers between devices: 6.91 us -> 6.47 us
    all_to_all x1, blocking collectives: 11.8 us -> 12.7 us  [shards(): parts = lax.all_to_all(summed, 'op', 0, 0, axis_index_groups=groups)]
    pallas_call x1, Pallas kernels: 2.94 us -> 2.03 us  [shards(): pl.pallas_call(functools.partial(terms_kernel, blocks), out_shape=jax.Sha...]
    pallas_call x1 -> x2, Pallas kernels: 1.6 us -> 2.22 us  [the longest x1 2.19 us: shards(): pl.pallas_call(functools.partial(ready_kernel, sec_devices), out_shape=(j...]
    ppermute x2, waiting for transfers between devices: 3.63 us -> 4.22 us  [exchange(): return lax.ppermute(value, axis, [(i, i ^ mask) for i in range(size)])]
    ppermute x2, starting transfers between devices: 6.91 us -> 6.47 us  [exchange(): return lax.ppermute(value, axis, [(i, i ^ mask) for i in range(size)])]
  transfers between devices with their start and end apart: 3 -> 3, of which waited for: 3 -> 2; matrix products, arithmetic and copies ran while one was open for 0% -> 0% of each run, Pallas kernels for 4% -> 5%
where the time goes in v8:
time: 41.8 us; the launch traced here: 41.5 us
  blocking collectives  24.8 us (59%)
  starting transfers between devices  6.47 us (15%)
  Pallas kernels  4.29 us (10%)
  waiting for transfers between devices  4.22 us (10%)
  local copies, waits for them, and re-layouts  0.84 us (2%)
  other arithmetic  0.73 us (2%)
    all_to_all x1, blocking collectives, shards(): parts = lax.all_to_all(summed, 'op', 0, 0, axis_index_groups=groups)  12.7 us
    all_to_all x1, blocking collectives, shards(): gathered = [lax.all_to_all(held, 'op', 0, 0, axis_index_groups=groups)]  12.1 us
    ppermute x2, starting transfers between devices, exchange(): return lax.ppermute(value, axis, [(i, i ^ mask) for i in range(size)])  6.47 us
    ppermute x2, waiting for transfers between devices, exchange(): return lax.ppermute(value, axis, [(i, i ^ mask) for i in range(size)])  4.22 us
    pallas_call x1, Pallas kernels, shards(): pl.pallas_call(functools.partial(ready_kernel, sec_devices), out_shape=(j...  2.19 us
    pallas_call x1, Pallas kernels, shards(): pl.pallas_call(functools.partial(terms_kernel, blocks), out_shape=jax.Sha...  2.03 us
  transfers between devices with their start and end apart: 3, of which 2 were waited for; matrix products, arithmetic and copies ran while one was open for 0% of the time, Pallas kernels for 5%

profile of v8, /device:TPU:0, one launch (start us, length us, event | category | flops | bytes accessed | tf_op | source)
XLA Modules:
  0.0 41.5 jit_solution(10242094753825360776)
XLA Ops:
  0.0 0.0 copy-start
  0.0 4.0 %collective-permute-start = (bf16[32,512]{1,0:T(8,128)(2,1)}, bf16[32,512]{1,0:T(8,128)(2,1)S(1)}, u32[]{:S(2)}, u32[]{:S(2)}) collective-permute-start(bf16[32,512]{1,0:T(8,128)(2,1)} %bitcast.4), channel_id=1, source_target_pairs={{0,16},{2,18},{4,20},{6,22},{8,24},{10,26},{12,28},{14,30},{16,0},... | collective-permute-start | bytes 98312 | tf_op jit(solution)/shard_map/ppermute | solution.py:20
  4.0 0.0 copy-start.1
  4.0 0.8 %copy-done.1 = bf16[1,32,512]{2,1,0:T(8,128)(2,1)S(1)} copy-done((bf16[1,32,512]{2,1,0:T(8,128)(2,1)S(1)}, bf16[1,32,512]{2,1,0:T(8,128)(2,1)}, u32[]{:S(2)}) %copy-start.1) | copy-done | bytes 32792
  4.8 0.0 copy-start.2
  4.8 0.0 copy-start.3
  4.9 1.6 %collective-permute-done = bf16[32,512]{1,0:T(8,128)(2,1)S(1)} collective-permute-done((bf16[32,512]{1,0:T(8,128)(2,1)}, bf16[32,512]{1,0:T(8,128)(2,1)S(1)}, u32[]{:S(2)}, u32[]{:S(2)}) %collective-permute-start) | collective-permute-done | bytes 32800 | tf_op jit(solution)/shard_map/ppermute | solution.py:20
  6.6 12.1 %all_to_all.10.source = bf16[8,64,512]{2,1,0:T(8,128)(2,1)S(1)} all-to-all(bf16[8,64,512]{2,1,0:T(8,128)(2,1)S(1)} %broadcast_in_dim.4), channel_id=1, replica_groups={{0,14,10,6,2,12,8,4},{16,30,26,22,18,28,24,20},{1,15,11,7,3,13,9,5},{17..., dimensions={0} | all-to-all | bytes 1048576 | tf_op jit(solution)/shard_map/all_to_all | solution.py:119
  18.7 0.0 collective-permute-start.1
  18.7 0.0 copy-done
  18.7 0.0 copy-done.2
  18.7 0.0 copy-done.3
  18.7 2.2 %shard_map.57 = (bf16[4,512,512]{2,1,0:T(8,128)(2,1)S(1)}, bf16[4,512,512]{2,1,0:T(8,128)(2,1)S(1)}) custom-call(s32[4]{0:T(128)S(1)} %copy-done.3, s32[2,16]{1,0:T(2,128)S(1)} %bitcast.6, bf16[4,512,512]{2,1,0:T(8,128)(2,1)S(1)} %copy-done, bf16[4,512,512]{2,1,0:T(8,128)(2,1)} %right_hbm.1, bf16[512,512]{1,0:T(8,128)(2,1)S(1)} %shard_map.56.own), custom_call_target="tpu_custom_call" | custom-call | bytes 4194304 | tf_op jit(solution)/shard_map/pallas_call | solution.py:132
  20.9 0.0 collective-permute-done.1.refs_0_
  20.9 2.0 %shard_map.58 = bf16[8,64,512]{2,1,0:T(8,128)(2,1)S(1)} custom-call(s32[4]{0:T(128)S(1)} %copy-done.3, s32[2,16]{1,0:T(2,128)S(1)} %bitcast.7, bf16[4,512,512]{2,1,0:T(8,128)(2,1)S(1)} %copy-done, bf16[4,512,512]{2,1,0:T(8,128)(2,1)S(1)} %get-tuple-element.7.right_ref, bf16[4,512,512]{2,1,0:T(8,128)(2,1)S(1)} %get-tuple-element.8.own_ref, ...), custom_call_target="tpu_custom_call" | custom-call | flops 2147483648 | bytes 4194304 | tf_op jit(solution)/shard_map/pallas_call | solution.py:142
  23.0 12.7 %all_to_all.11 = bf16[8,64,512]{2,1,0:T(8,128)(2,1)S(1)} all-to-all(bf16[8,64,512]{2,1,0:T(8,128)(2,1)S(1)} %shard_map.58), channel_id=1, replica_groups={{0,14,10,6,2,12,8,4},{16,30,26,22,18,28,24,20},{1,15,11,7,3,13,9,5},{17..., dimensions={0} | all-to-all | bytes 1048576 | tf_op jit(solution)/shard_map/all_to_all | solution.py:155
  35.7 0.1 convert_reduce_fusion
  35.8 2.4 %collective-permute-start.2 = (bf16[32,512]{1,0:T(8,128)(2,1)S(1)}, bf16[32,512]{1,0:T(8,128)(2,1)S(1)}, u32[]{:S(2)}, u32[]{:S(2)}) collective-permute-start(bf16[32,512]{1,0:T(8,128)(2,1)S(1)} %select_convert_fusion), channel_id=1, source_target_pairs={{0,16},{2,18},{4,20},{6,22},{8,24},{10,26},{12,28},{14,30},{16,0},... | collective-permute-start | bytes 98312 | tf_op jit(solution)/shard_map/ppermute | solution.py:20
  38.3 2.6 %collective-permute-done.2 = bf16[32,512]{1,0:T(8,128)(2,1)S(1)} collective-permute-done((bf16[32,512]{1,0:T(8,128)(2,1)S(1)}, bf16[32,512]{1,0:T(8,128)(2,1)S(1)}, u32[]{:S(2)}, u32[]{:S(2)}) %collective-permute-start.2) | collective-permute-done | bytes 32800 | tf_op jit(solution)/shard_map/ppermute | solution.py:20
  40.9 0.6 %fusion = bf16[1,32,512]{2,1,0:T(8,128)(2,1)} fusion(bf16[32,512]{1,0:T(8,128)(2,1)S(1)} %collective-permute-done.2, f32[64,512]{1,0:T(8,128)S(1)} %convert_reduce_fusion, pred[]{:T(512)S(6)} %ne.4), kind=kLoop, calls=%fused_computation.4 | loop fusion | flops 81920 | bytes 196609 | tf_op jit(solution)/shard_map/broadcast_in_dim | solution.py:163
  (6 shorter events, 0.1 us)
Async XLA Ops:
  0.0 18.7 %copy-start = (bf16[4,512,512]{2,1,0:T(8,128)(2,1)S(1)}, bf16[4,512,512]{2,1,0:T(8,128)(2,1)}, u32[]{:S(2)}) copy-start(bf16[4,512,512]{2,1,0:T(8,128)(2,1)} %left_ref.3) | copy-start | bytes 6291460
  0.0 6.5 %collective-permute-start = (bf16[32,512]{1,0:T(8,128)(2,1)}, bf16[32,512]{1,0:T(8,128)(2,1)S(1)}, u32[]{:S(2)}, u32[]{:S(2)}) collective-permute-start(bf16[32,512]{1,0:T(8,128)(2,1)} %bitcast.4), channel_id=1, source_target_pairs={{0,16},{2,18},{4,20},{6,22},{8,24},{10,26},{12,28},{14,30},{16,0},... | collective-permute-start | bytes 98312 | tf_op jit(solution)/shard_map/ppermute | solution.py:20
  4.0 0.8 %copy-start.1 = (bf16[1,32,512]{2,1,0:T(8,128)(2,1)S(1)}, bf16[1,32,512]{2,1,0:T(8,128)(2,1)}, u32[]{:S(2)}) copy-start(bf16[1,32,512]{2,1,0:T(8,128)(2,1)} %param.5) | copy-start | bytes 98308
  4.8 13.9 %copy-start.2 = (s32[16,2]{0,1:T(2,128)S(1)}, s32[16,2]{0,1:T(2,128)}, u32[]{:S(2)}) copy-start(s32[16,2]{0,1:T(2,128)} %param.9) | copy-start | bytes 388
  4.8 13.9 %copy-start.3 = (s32[4]{0:T(128)S(1)}, s32[4]{0:T(128)}, u32[]{:S(2)}) copy-start(s32[4]{0:T(128)} %sector_ref.3) | copy-start | bytes 52
  18.7 2.3 %collective-permute-start.1 = (bf16[8,64,512]{2,1,0:T(8,128)(2,1)S(1)}, bf16[8,64,512]{2,1,0:T(8,128)(2,1)S(1)}, u32[]{:S(2)}, u32[]{:S(2)}) collective-permute-start(bf16[8,64,512]{2,1,0:T(8,128)(2,1)S(1)} %all_to_all.10.source), channel_id=1, source_target_pairs={{0,1},{1,0},{2,3},{3,2},{4,5},{5,4},{6,7},{7,6},{8,9},{9,8},{10,11... | collective-permute-start | bytes 1572872 | tf_op jit(solution)/shard_map/ppermute | solution.py:122
  35.8 5.0 %collective-permute-start.2 = (bf16[32,512]{1,0:T(8,128)(2,1)S(1)}, bf16[32,512]{1,0:T(8,128)(2,1)S(1)}, u32[]{:S(2)}, u32[]{:S(2)}) collective-permute-start(bf16[32,512]{1,0:T(8,128)(2,1)S(1)} %select_convert_fusion), channel_id=1, source_target_pairs={{0,16},{2,18},{4,20},{6,22},{8,24},{10,26},{12,28},{14,30},{16,0},... | collective-permute-start | bytes 98312 | tf_op jit(solution)/shard_map/ppermute | solution.py:20
